TPU v7x, 256 devices: a whole 4x4x8 slice. The times are simulated.
256 devices in a mesh: fft: 32 (over z, y), grp: 8 (over x, core).
Axes of the slice: x: 4, y: 4, z: 8, core: 2. Of those that a mesh axis runs over, the one named last changes fastest.
Arguments:
- root_density: float32 [768, 768, 128], P('fft', 'grp'), may hold values from -8 to 8
- patch_fluid: float32 [5, 12, 12, 12, 8192], P(None, None, None, None, ('fft', 'grp')), may hold values from -5 to 60, as said below
- ghost_list: int32 [2, 256, 64], P(None, ('fft', 'grp')), may hold values from -1 to 4607, as said below
Outputs:
- root_potential: float32 [768, 768, 128], P('fft', 'grp')
- fine_potential: float32 [8, 8, 8, 8192], P(None, None, None, ('fft', 'grp'))
- fluid_next: float32 [5, 8, 8, 8, 8192], P(None, None, None, None, ('fft', 'grp'))
Inputs may be any that keep to these rules, and one draw needn't show every extreme that they name: `ghost_list`: Every slot of every device is named exactly once, no two patches share a corner, every device receives exactly 2 patches from some one sender, and every sending device uses its last corner in some column. `patch_fluid`: density and pressure are positive in every cell.
All inputs are finite; a program needn't handle non-finite values.
Results may differ from a plain program's by a relative error of at most 0.0003.
Values sent between devices are 32-bit elements; how exact they have to be, the bound alone decides.
A program may use at most 192 MiB of HBM per device.

v0:
```python
import math

import jax
import jax.numpy as jnp
import numpy as np
from jax import lax
from jax.sharding import PartitionSpec as P

SWEEPS = 8


GAMMA = 5.0 / 3.0
SCREEN = 0.0006
OMEGA = 1.5
COURANT = 0.4
FINE_STEP = 0.5
HIGH = lax.Precision.HIGHEST


def with_halo(cells, sides, width):
    for axis, dim in sides:
        count = lax.axis_size(axis)
        ends = count - 1
        head = lax.slice_in_dim(cells, 0, width, axis=dim)
        tail = lax.slice_in_dim(cells, cells.shape[dim] - width, cells.shape[dim], axis=dim)
        cells = jnp.concatenate(
            [
                lax.ppermute(tail, axis, [(i, (i + 1) % count) for i in range(ends)]),
                cells,
                lax.ppermute(head, axis, [((i + 1) % count, i) for i in range(ends)]),
            ],
            axis=dim,
        )
    return cells


def sine_table(count):
    index = jnp.arange(count, dtype=jnp.int32) + 1
    phase = index[:, None] * index[None, :] % (2 * (count + 1))
    return math.sqrt(2.0 / (count + 1)) * jnp.sin(jnp.pi * phase.astype(jnp.float32) / (count + 1))


def eigen(count, index):
    half = jnp.sin(jnp.pi * (index + 1).astype(jnp.float32) / (2 * (count + 1)))
    return 4.0 * half * half


def spread_table():
    table = np.zeros((10, 6), np.float32)
    for fine in range(10):
        where_at = fine / 2.0 + 0.25
        lower = int(np.floor(where_at))
        frac = where_at - lower
        table[fine, lower] += 1.0 - frac
        table[fine, lower + 1] += frac
    return table


def block_offsets(stride_y, stride_z):
    cube = jnp.arange(6, dtype=jnp.int32)
    return (
        (cube[:, None, None] * stride_y + cube[None, :, None]) * stride_z + cube[None, None, :]
    ).reshape(-1)


def primitives(fluid):
    dens = fluid[0]
    vel = fluid[1:4] / dens
    kinetic = 0.5 * jnp.sum(fluid[1:4] * vel, axis=0)
    pres = (GAMMA - 1.0) * (fluid[4] - kinetic)
    return (dens, vel, pres)


def signal_speed(fluid):
    dens, vel, pres = primitives(fluid[:, 2:10, 2:10, 2:10])
    sound = jnp.sqrt(GAMMA * pres / dens)
    return jnp.max(jnp.max(jnp.abs(vel), axis=0) + sound)


def along(array, axis, start, stop):
    return lax.slice_in_dim(array, start, stop, axis=axis + 1)


def conserved_flux(state, axis):
    dens = state[0]
    vel = state[1:4]
    pres = state[4]
    normal = vel[axis]
    energy = pres / (GAMMA - 1.0) + 0.5 * dens * jnp.sum(vel * vel, axis=0)
    cons = jnp.stack([dens, dens * vel[0], dens * vel[1], dens * vel[2], energy])
    moment = [dens * normal * vel[other] + (pres if other == axis else 0.0) for other in range(3)]
    flux = jnp.stack([dens * normal, moment[0], moment[1], moment[2], (energy + pres) * normal])
    speed = jnp.abs(normal) + jnp.sqrt(GAMMA * pres / dens)
    return (cons, flux, speed)


def flux_difference(prim, axis):
    for other in range(3):
        if other != axis:
            prim = along(prim, other, 2, 10)
    left_diff = along(prim, axis, 1, 11) - along(prim, axis, 0, 10)
    right_diff = along(prim, axis, 2, 12) - along(prim, axis, 1, 11)
    slope = (
        0.5
        * (jnp.sign(left_diff) + jnp.sign(right_diff))
        * jnp.minimum(jnp.abs(left_diff), jnp.abs(right_diff))
    )
    centre = along(prim, axis, 1, 11)
    upper = centre + 0.5 * slope
    lower = centre - 0.5 * slope
    cons_left, flux_left, speed_left = conserved_flux(along(upper, axis, 0, 9), axis)
    cons_right, flux_right, speed_right = conserved_flux(along(lower, axis, 1, 10), axis)
    flux = 0.5 * (flux_left + flux_right) - 0.5 * jnp.maximum(speed_left, speed_right) * (
        cons_right - cons_left
    )
    return along(flux, axis, 1, 9) - along(flux, axis, 0, 8)


def advance(fluid, field, step):
    dens, vel, pres = primitives(fluid)
    prim = jnp.concatenate([dens[None], vel, pres[None]], axis=0)
    change = flux_difference(prim, 0) + flux_difference(prim, 1) + flux_difference(prim, 2)
    inner = fluid[:, 2:10, 2:10, 2:10]
    moved = inner - step / FINE_STEP * change
    pull = -jnp.stack(
        [
            field[2:, 1:-1, 1:-1] - field[:-2, 1:-1, 1:-1],
            field[1:-1, 2:, 1:-1] - field[1:-1, :-2, 1:-1],
            field[1:-1, 1:-1, 2:] - field[1:-1, 1:-1, :-2],
        ]
    ) / (2.0 * FINE_STEP)
    momenta = moved[1:4] + step * inner[0] * pull
    energy = moved[4] + step * jnp.sum(inner[1:4] * pull, axis=0)
    return jnp.concatenate([moved[0:1], momenta, energy[None]], axis=0)


def spread(coarse, count):
    table = jnp.asarray(spread_table())
    block = coarse.reshape(6, 6, 6, count)
    block = jnp.einsum("ia,abcp->ibcp", table, block, precision=HIGH)
    block = jnp.einsum("jb,ibcp->ijcp", table, block, precision=HIGH)
    return jnp.einsum("kc,ijcp->ijkp", table, block, precision=HIGH)


def relax(field, dens):
    index = jnp.arange(8, dtype=jnp.int32)
    parity = (index[:, None, None] + index[None, :, None] + index[None, None, :]) % 2
    scale = 1.0 / (6.0 + SCREEN * FINE_STEP * FINE_STEP)
    for sweep in range(SWEEPS):
        for colour in (0, 1):
            near = (
                field[2:, 1:-1, 1:-1]
                + field[:-2, 1:-1, 1:-1]
                + field[1:-1, 2:, 1:-1]
                + field[1:-1, :-2, 1:-1]
                + field[1:-1, 1:-1, 2:]
                + field[1:-1, 1:-1, :-2]
            )
            inner = field[1:-1, 1:-1, 1:-1]
            moved = (1.0 - OMEGA) * inner + OMEGA * scale * (near - FINE_STEP * FINE_STEP * dens)
            inner = jnp.where((parity == colour)[..., None], moved, inner)
            field = field.at[1:-1, 1:-1, 1:-1].set(inner)
    return field


def refine(fluid, coarse, step):
    count = fluid.shape[-1]
    field = relax(spread(coarse, count), fluid[0, 2:10, 2:10, 2:10])
    return (field[1:-1, 1:-1, 1:-1], advance(fluid, field, step))


def per_device(root_density, patch_fluid, ghost_list):
    size_x, size_y, size_z = root_density.shape
    count_fft = lax.axis_size("fft")
    count_grp = lax.axis_size("grp")
    fft_pos = lax.axis_index("fft")
    grp_pos = lax.axis_index("grp")
    width_x = size_x * count_fft
    width_y = size_y * count_grp
    count = patch_fluid.shape[-1]
    speed = lax.pmax(signal_speed(patch_fluid), ("fft", "grp"))
    step = COURANT * FINE_STEP / speed
    table_x = sine_table(width_x)
    table_y = sine_table(width_y)
    table_z = sine_table(size_z)
    eigen_z = eigen(size_z, jnp.arange(size_z, dtype=jnp.int32))[None, None, :]
    spec = jnp.einsum("xyz,kz->xyk", root_density, table_z, precision=HIGH)
    lines = lax.all_to_all(spec, "fft", split_axis=1, concat_axis=0, tiled=True)
    lines = jnp.einsum("kx,xyz->kyz", table_x, lines, precision=HIGH)
    columns = lax.all_to_all(
        lax.all_to_all(lines, "fft", split_axis=0, concat_axis=1, tiled=True),
        "grp",
        split_axis=0,
        concat_axis=1,
        tiled=True,
    )
    columns = jnp.einsum("ky,xyz->xkz", table_y, columns, precision=HIGH)
    rows_x = (
        fft_pos * size_x
        + grp_pos * (size_x // count_grp)
        + jnp.arange(size_x // count_grp, dtype=jnp.int32)
    )
    total = (
        eigen(width_x, rows_x)[:, None, None]
        + eigen(width_y, jnp.arange(width_y, dtype=jnp.int32))[None, :, None]
        + eigen_z
        + SCREEN
    )
    columns = -columns / total
    columns = jnp.einsum("ky,xyz->xkz", table_y, columns, precision=HIGH)
    lines = lax.all_to_all(
        lax.all_to_all(columns, "grp", split_axis=1, concat_axis=0, tiled=True),
        "fft",
        split_axis=1,
        concat_axis=0,
        tiled=True,
    )
    lines = jnp.einsum("kx,xyz->kyz", table_x, lines, precision=HIGH)
    spec = lax.all_to_all(lines, "fft", split_axis=0, concat_axis=1, tiled=True)
    potential = jnp.einsum("xyz,kz->xyk", spec, table_z, precision=HIGH)
    framed = with_halo(potential, (("fft", 0), ("grp", 1)), 1)
    framed = jnp.pad(framed, ((0, 0), (0, 0), (1, 1)))
    per_z = size_z // 4
    per_y = size_y // 4
    code = jnp.maximum(ghost_list[0, 0], 0)
    slot = ghost_list[1, 0]
    start_x = 4 * (code // (per_y * per_z))
    start_y = 4 * (code // per_z % per_y)
    start_z = 4 * (code % per_z)
    start = (start_x * (size_y + 2) + start_y) * (size_z + 2) + start_z
    offsets = block_offsets(size_y + 2, size_z + 2)
    blocks = framed.reshape(-1)[start[None, :] + offsets[:, None]]
    arrived, arrived_slot = (
        lax.all_to_all(blocks, "fft", split_axis=1, concat_axis=1, tiled=True),
        lax.all_to_all(slot[None, :], "fft", split_axis=1, concat_axis=1, tiled=True),
    )
    placing = (arrived_slot[0][:, None] == jnp.arange(count, dtype=jnp.int32)[None, :]).astype(
        jnp.float32
    )
    coarse = jnp.dot(arrived, placing, precision=HIGH)
    fine, fluid_next = refine(patch_fluid, coarse, step)
    return (potential, fine, fluid_next)


def solution(mesh):
    return jax.shard_map(
        per_device,
        mesh=mesh,
        in_specs=(
            P("fft", "grp", None),
            P(None, None, None, None, ("fft", "grp")),
            P(None, ("fft", "grp"), None),
        ),
        out_specs=(
            P("fft", "grp", None),
            P(None, None, None, ("fft", "grp")),
            P(None, None, None, None, ("fft", "grp")),
        ),
        check_vma=False,
    )
```

profile of v0, /device:TPU:1, one launch (start us, length us, event | category | flops | bytes accessed | tf_op | source)
XLA Modules:
  0.0 539.9 jit_solution(6551779289861281566)
XLA Ops:
  3.3 1.7 copy.56
  5.0 12.5 %all-to-all-start = ((f32[24,96,128]{2,0,1:T(8,128)}), f32[24,96,128]{2,0,1:T(8,128)S(1)}, u32[]{:S(2)}, u32[]{:S(2)}) async-start(f32[24,96,128]{2,0,1:T(8,128)} %copy.56), calls=%async_computation | async-start | bytes 2359296 | tf_op jit(solution)/shard_map/all_to_all | solution.py:188
  19.1 2.9 multiply_reduce_fusion
  32.4 2.5 fusion.2
  42.3 3.4 all-to-all-done
  45.8 12.9 %fusion.17 = f32[768,3,128]{2,0,1:T(8,128)S(1)} fusion(f32[768,3,128]{2,0,1:T(8,128)S(1)} %bitcast.229, s32[768]{0:T(1024)S(1)} %iota_add_fusion.2), kind=kOutput, calls=%fused_computation.31 | convolution fusion | flops 2723807232 | bytes 2362368 | tf_op jit(solution)/shard_map/kx,xyz->kyz/dot_general | solution.py:189
  58.7 2.0 copy.58
  60.7 6.8 %all-to-all-start.1 = ((f32[768,3,128]{2,1,0:T(4,128)}), f32[768,3,128]{2,1,0:T(4,128)}, u32[]{:S(2)}, u32[]{:S(2)}) async-start(f32[768,3,128]{2,1,0:T(4,128)} %copy.58), calls=%async_computation.1 | async-start | bytes 3145728 | tf_op jit(solution)/shard_map/all_to_all | solution.py:191
  67.5 2.9 add_dynamic-update-slice_fusion.1
  70.4 2.8 multiply_dynamic-update-slice_fusion
  79.0 24.2 %all-to-all-done.1 = f32[768,3,128]{2,1,0:T(4,128)} async-done(((f32[768,3,128]{2,1,0:T(4,128)}), f32[768,3,128]{2,1,0:T(4,128)}, u32[]{:S(2)}, u32[]{:S(2)}) %all-to-all-start.1) | async-done | bytes 1179680 | tf_op jit(solution)/shard_map/all_to_all | solution.py:191
  106.1 8.9 %all-to-all-start.2 = ((f32[24,96,128]{2,1,0:T(8,128)}), f32[24,96,128]{2,1,0:T(8,128)}, u32[]{:S(2)}, u32[]{:S(2)}) async-start(f32[24,96,128]{2,1,0:T(8,128)} %copy.61), calls=%async_computation.2 | async-start | bytes 2359296 | tf_op jit(solution)/shard_map/all_to_all | solution.py:190
  118.3 13.1 %all-to-all-done.2 = f32[24,96,128]{2,1,0:T(8,128)} async-done(((f32[24,96,128]{2,1,0:T(8,128)}), f32[24,96,128]{2,1,0:T(8,128)}, u32[]{:S(2)}, u32[]{:S(2)}) %all-to-all-start.2) | async-done | bytes 1179680 | tf_op jit(solution)/shard_map/all_to_all | solution.py:190
  132.8 14.9 %fusion.31 = f32[3,768,128]{1,2,0:T(8,128)S(1)} fusion(f32[3,768,128]{2,1,0:T(8,128)S(1)} %bitcast.230, s32[768]{0:T(1024)S(1)} %iota_add_fusion.2), kind=kOutput, calls=%fused_computation.53 | convolution fusion | flops 2724102144 | bytes 2362368 | tf_op jit(solution)/shard_map/ky,xyz->xkz/dot_general | solution.py:197
  147.7 12.6 %fusion.25 = f32[3,768,128]{1,2,0:T(8,128)S(1)} fusion(f32[3,768,128]{1,2,0:T(8,128)S(1)} %fusion.31, s32[768]{0:T(1024)S(1)} %iota_add_fusion.2, f32[128]{0:T(128)S(1)} %multiply_multiply_fusion.4, f32[3,768]{1,0:T(4,128)S(1)} %broadcast_add_fusion), kind=kOutput, calls=%fused_computation.51 | convolution fusion | flops 2724691968 | bytes 2372096 | tf_op jit(solution)/shard_map/ky,xyz->xkz/dot_general | solution.py:210
  161.9 5.2 all-to-all-start.3
  171.1 16.8 %all-to-all-done.3 = f32[3,768,128]{2,0,1:T(4,128)} async-done(((f32[3,768,128]{2,0,1:T(4,128)}), f32[3,768,128]{2,0,1:T(4,128)}, u32[]{:S(2)}, u32[]{:S(2)}) %all-to-all-start.3) | async-done | bytes 1179680 | tf_op jit(solution)/shard_map/all_to_all | solution.py:212
  191.2 5.7 %all-to-all-start.4 = ((f32[24,96,128]{2,0,1:T(8,128)}), f32[24,96,128]{2,0,1:T(8,128)}, u32[]{:S(2)}, u32[]{:S(2)}) async-start(f32[24,96,128]{2,0,1:T(8,128)} %copy.67), calls=%async_computation.4 | async-start | bytes 2359296 | tf_op jit(solution)/shard_map/all_to_all | solution.py:211
  198.5 1.8 slice_bitcast_fusion
  201.2 2.2 multiply_dynamic-update-slice_fusion.28
  203.3 2.0 multiply_dynamic-update-slice_fusion.20
  205.3 2.1 multiply_dynamic-update-slice_fusion.10
  210.0 15.4 %all-to-all-done.4 = f32[24,96,128]{2,0,1:T(8,128)} async-done(((f32[24,96,128]{2,0,1:T(8,128)}), f32[24,96,128]{2,0,1:T(8,128)}, u32[]{:S(2)}, u32[]{:S(2)}) %all-to-all-start.4) | async-done | bytes 1179680 | tf_op jit(solution)/shard_map/all_to_all | solution.py:211
  226.7 13.2 %fusion.11 = f32[768,3,128]{2,0,1:T(8,128)S(1)} fusion(f32[768,3,128]{2,0,1:T(8,128)S(1)} %bitcast.228, s32[768]{0:T(1024)S(1)} %iota_add_fusion.2), kind=kOutput, calls=%fused_computation.28 | convolution fusion | flops 2723807232 | bytes 2362368 | tf_op jit(solution)/shard_map/kx,xyz->kyz/dot_general | solution.py:218
  239.9 2.0 copy.69
  241.9 7.0 %all-to-all-start.5 = ((f32[768,3,128]{2,1,0:T(4,128)}), f32[768,3,128]{2,1,0:T(4,128)}, u32[]{:S(2)}, u32[]{:S(2)}) async-start(f32[768,3,128]{2,1,0:T(4,128)} %copy.69), calls=%async_computation.5 | async-start | bytes 3145728 | tf_op jit(solution)/shard_map/all_to_all | solution.py:219
  250.6 2.5 multiply_dynamic-update-slice_fusion.27
  258.0 4.2 multiply_subtract_fusion.2
  262.2 5.2 multiply_subtract_fusion
  267.4 17.3 %all-to-all-done.5 = f32[768,3,128]{2,1,0:T(4,128)} async-done(((f32[768,3,128]{2,1,0:T(4,128)}), f32[768,3,128]{2,1,0:T(4,128)}, u32[]{:S(2)}, u32[]{:S(2)}) %all-to-all-start.5) | async-done | bytes 1179680 | tf_op jit(solution)/shard_map/all_to_all | solution.py:219
  284.7 7.3 %all-to-all-start.7 = ((s32[1,32,2]{2,0,1:T(1,128)}), s32[1,32,2]{2,0,1:T(1,128)S(1)}, u32[]{:S(2)}, u32[]{:S(2)}) async-start(s32[1,32,2]{2,0,1:T(1,128)} %bitcast.30), calls=%async_computation.7 | async-start | bytes 32768 | tf_op jit(solution)/shard_map/all_to_all | solution.py:235
  295.0 3.1 collective-permute-start
  299.5 3.8 collective-permute-done.1
  303.3 6.2 %collective-permute-start.2 = (f32[26,1,128]{2,1,0:T(1,128)S(1)}, f32[26,1,128]{2,1,0:T(1,128)S(1)}, u32[]{:S(2)}, u32[]{:S(2)}) collective-permute-start(f32[26,1,128]{2,1,0:T(1,128)S(1)} %get-tuple-element.261), channel_id=1, source_target_pairs={{0,1},{1,2},{2,3},{3,4},{4,5},{5,6},{6,7},{8,9},{9,10},{10,11},{11... | collective-permute-start | bytes 39944 | tf_op jit(solution)/shard_map/ppermute | solution.py:28
  309.6 1.9 collective-permute-start.3
  311.5 3.1 collective-permute-done.3
  314.6 2.4 select_maximum_fusion
  317.0 3.2 reshape.888
  320.2 71.2 %gather_fusion = f32[13824]{0:T(1024)S(1)} fusion(f32[331240]{0:T(1024)S(1)} %reshape.888, s32[14336]{0:T(1024)S(1)} %pad_clamp_fusion), kind=kCustom, calls=%fused_computation | custom fusion | bytes 165888 | tf_op jit(solution)/shard_map/gather | solution.py:232
  391.4 5.3 all_to_all.114
  396.7 3.8 copy.73
  400.5 11.5 %all-to-all-start.6 = ((f32[216,32,2]{0,2,1:T(2,128)}), f32[216,32,2]{0,2,1:T(2,128)S(1)}, u32[]{:S(2)}, u32[]{:S(2)}) async-start(f32[216,32,2]{0,2,1:T(2,128)} %copy.73), calls=%async_computation.6 | async-start | bytes 131072 | tf_op jit(solution)/shard_map/all_to_all | solution.py:234
  413.3 7.5 %all-to-all-done.6 = f32[216,32,2]{0,2,1:T(2,128)S(1)} async-done(((f32[216,32,2]{0,2,1:T(2,128)}), f32[216,32,2]{0,2,1:T(2,128)S(1)}, u32[]{:S(2)}, u32[]{:S(2)}) %all-to-all-start.6) | async-done | bytes 55328 | tf_op jit(solution)/shard_map/all_to_all | solution.py:234
  450.5 1.9 multiply_reduce_fusion.2
  452.4 2.0 fusion.153
  454.4 4.2 multiply_subtract_fusion.1
  458.6 72.9 %pmax.7 = f32[]{:T(128)} all-reduce(f32[]{:T(128)} %fusion.153), channel_id=1, replica_groups=mesh['fft'=32,'grp'=8] {'fft','grp'}, use_global_device_ids=true, to_apply=%region_3.0 | all-reduce | flops 1 | bytes 8 | tf_op jit(solution)/shard_map/pmax | solution.py:181
  533.3 4.5 fusion.36
  (202 shorter events, 95.2 us)
Async XLA Ops:
  0.6 1.3 copy-start
  5.0 40.7 %all-to-all-start = ((f32[24,96,128]{2,0,1:T(8,128)}), f32[24,96,128]{2,0,1:T(8,128)S(1)}, u32[]{:S(2)}, u32[]{:S(2)}) async-start(f32[24,96,128]{2,0,1:T(8,128)} %copy.56), calls=%async_computation | async-start | bytes 2359296 | tf_op jit(solution)/shard_map/all_to_all | solution.py:188
  24.2 8.2 %copy-start.2 = (f32[5,12,12,12,32]{4,3,2,1,0:T(8,128)}, f32[5,12,12,12,32]{4,3,2,1,0:T(8,128)S(1)}, u32[]{:S(2)}) copy-start(f32[5,12,12,12,32]{4,3,2,1,0:T(8,128)S(1)} %pad_maximum_fusion) | copy-start | bytes 3317764
  25.3 3.6 copy-start.9
  25.3 4.5 copy-start.16
  34.9 3.8 copy-start.6
  34.9 4.7 copy-start.3
  39.6 1.5 copy-start.24
  60.7 14.3 %slice-start = ((s8[5898240]{0:T(1024)(128)(4,1)}), s8[1703936]{0:T(1024)(128)(4,1)S(1)}, s32[]{:S(2)}) async-start(s8[5898240]{0:T(1024)(128)(4,1)} %bitcast.219), calls=%async_computation.8 | async-start | bytes 3407872
  60.7 42.6 %all-to-all-start.1 = ((f32[768,3,128]{2,1,0:T(4,128)}), f32[768,3,128]{2,1,0:T(4,128)}, u32[]{:S(2)}, u32[]{:S(2)}) async-start(f32[768,3,128]{2,1,0:T(4,128)} %copy.58), calls=%async_computation.1 | async-start | bytes 3145728 | tf_op jit(solution)/shard_map/all_to_all | solution.py:191
  67.5 7.4 %slice-start.1 = ((s8[5898240]{0:T(1024)(128)(4,1)}), s8[4194304]{0:T(1024)(128)(4,1)S(1)}, s32[]{:S(2)}) async-start(s8[5898240]{0:T(1024)(128)(4,1)} %bitcast.219), calls=%async_computation.9 | async-start | bytes 8388608
  70.4 3.6 copy-start.10
  70.4 3.6 copy-start.17
  76.6 1.2 copy-start.12
  76.6 2.2 copy-start.18
  76.6 2.2 copy-start.35
  106.1 9.0 %copy-start.13 = (f32[5,8,10,8,32]{4,3,2,1,0:T(8,128)S(1)}, f32[5,8,10,8,32]{4,3,2,1,0:T(8,128)}, u32[]{:S(2)}) copy-start(f32[5,8,10,8,32]{4,3,2,1,0:T(8,128)} %copy-done.12) | copy-start | bytes 1228804
  106.1 25.3 %all-to-all-start.2 = ((f32[24,96,128]{2,1,0:T(8,128)}), f32[24,96,128]{2,1,0:T(8,128)}, u32[]{:S(2)}, u32[]{:S(2)}) async-start(f32[24,96,128]{2,1,0:T(8,128)} %copy.61), calls=%async_computation.2 | async-start | bytes 2359296 | tf_op jit(solution)/shard_map/all_to_all | solution.py:190
  161.8 5.9 %copy-start.19 = (f32[5,8,10,8,32]{4,3,2,1,0:T(8,128)S(1)}, f32[5,8,10,8,32]{4,3,2,1,0:T(8,128)}, u32[]{:S(2)}) copy-start(f32[5,8,10,8,32]{4,3,2,1,0:T(8,128)} %copy-done.18) | copy-start | bytes 1228804
  161.9 26.0 %all-to-all-start.3 = ((f32[3,768,128]{2,0,1:T(4,128)}), f32[3,768,128]{2,0,1:T(4,128)}, u32[]{:S(2)}, u32[]{:S(2)}) async-start(f32[3,768,128]{2,0,1:T(4,128)} %copy.64), calls=%async_computation.3 | async-start | bytes 3145728 | tf_op jit(solution)/shard_map/all_to_all | solution.py:212
  191.2 9.1 %copy-start.11 = (f32[5,10,8,8,32]{4,3,2,1,0:T(8,128)S(1)}, f32[5,10,8,8,32]{4,3,2,1,0:T(8,128)}, u32[]{:S(2)}) copy-start(f32[5,10,8,8,32]{4,3,2,1,0:T(8,128)} %copy-done.9) | copy-start | bytes 1228804
  191.2 34.2 %all-to-all-start.4 = ((f32[24,96,128]{2,0,1:T(8,128)}), f32[24,96,128]{2,0,1:T(8,128)}, u32[]{:S(2)}, u32[]{:S(2)}) async-start(f32[24,96,128]{2,0,1:T(8,128)} %copy.67), calls=%async_computation.4 | async-start | bytes 2359296 | tf_op jit(solution)/shard_map/all_to_all | solution.py:211
  201.2 4.2 copy-start.14
  203.3 5.0 copy-start.29
  205.3 3.9 copy-start.7
  207.4 2.0 copy-start.4
  241.9 7.1 %copy-start.33 = (s32[216,64,1]{1,0,2:T(8,128)S(1)}, s32[216,64,1]{1,0,2:T(8,128)}, u32[]{:S(2)}) copy-start(s32[216,64,1]{1,0,2:T(8,128)} %compare_select_fusion) | copy-start | bytes 165892
  241.9 42.8 %all-to-all-start.5 = ((f32[768,3,128]{2,1,0:T(4,128)}), f32[768,3,128]{2,1,0:T(4,128)}, u32[]{:S(2)}, u32[]{:S(2)}) async-start(f32[768,3,128]{2,1,0:T(4,128)} %copy.69), calls=%async_computation.5 | async-start | bytes 3145728 | tf_op jit(solution)/shard_map/all_to_all | solution.py:219
  249.7 3.3 copy-start.20
  250.6 2.5 copy-start.15
  250.6 2.5 copy-start.28
  253.1 2.1 copy-start.5
  254.2 2.1 copy-start.8
  256.3 1.6 copy-start.27
  257.9 4.2 copy-start.23
  257.9 4.2 copy-start.25
  284.7 115.8 %all-to-all-start.7 = ((s32[1,32,2]{2,0,1:T(1,128)}), s32[1,32,2]{2,0,1:T(1,128)S(1)}, u32[]{:S(2)}, u32[]{:S(2)}) async-start(s32[1,32,2]{2,0,1:T(1,128)} %bitcast.30), calls=%async_computation.7 | async-start | bytes 32768 | tf_op jit(solution)/shard_map/all_to_all | solution.py:235
  295.0 22.1 %copy-start.22 = (f32[24,96,128]{2,1,0:T(8,128)}, f32[24,96,128]{2,1,0:T(8,128)S(1)}, u32[]{:S(2)}) copy-start(f32[24,96,128]{2,1,0:T(8,128)S(1)} %fusion.39) | copy-start | bytes 3538948
  295.0 4.5 collective-permute-start
  298.1 5.1 collective-permute-start.1
  303.3 8.2 %collective-permute-start.2 = (f32[26,1,128]{2,1,0:T(1,128)S(1)}, f32[26,1,128]{2,1,0:T(1,128)S(1)}, u32[]{:S(2)}, u32[]{:S(2)}) collective-permute-start(f32[26,1,128]{2,1,0:T(1,128)S(1)} %get-tuple-element.261), channel_id=1, source_target_pairs={{0,1},{1,2},{2,3},{3,4},{4,5},{5,6},{6,7},{8,9},{9,10},{10,11},{11... | collective-permute-start | bytes 39944 | tf_op jit(solution)/shard_map/ppermute | solution.py:28
  309.6 5.0 collective-permute-start.3
  400.5 20.3 %all-to-all-start.6 = ((f32[216,32,2]{0,2,1:T(2,128)}), f32[216,32,2]{0,2,1:T(2,128)S(1)}, u32[]{:S(2)}, u32[]{:S(2)}) async-start(f32[216,32,2]{0,2,1:T(2,128)} %copy.73), calls=%async_computation.6 | async-start | bytes 131072 | tf_op jit(solution)/shard_map/all_to_all | solution.py:234
  413.3 9.1 %copy-start.34 = (f32[10,6,1,1]{0,1,3,2:T(8,128)S(1)}, f32[10,6,1,1]{0,1,3,2:T(8,128)}, u32[]{:S(2)}) copy-start(f32[10,6,1,1]{0,1,3,2:T(8,128)} %constant.549) | copy-start | bytes 724
  449.5 2.9 copy-start.32
  450.5 3.9 copy-start.30
  454.4 78.9 %copy-start.21 = (f32[5,9,8,8,32]{4,3,2,1,0:T(8,128)S(1)}, f32[5,9,8,8,32]{4,3,2,1,0:T(8,128)}, u32[]{:S(2)}) copy-start(f32[5,9,8,8,32]{4,3,2,1,0:T(8,128)} %multiply_subtract_fusion.2) | copy-start | bytes 1105924
  538.0 1.7 copy-start.1
  (2 other events, 2.2 us)
where the time goes:
time: 545 us; the launch traced here: 540 us
  local copies, waits for them, and re-layouts  124 us (23%)
  waiting for transfers between devices  105 us (19%)
  other arithmetic  99.6 us (18%)
  starting transfers between devices  77.6 us (14%)
  blocking collectives  72.9 us (13%)
  matrix products  58.6 us (11%)
    pmax x1, blocking collectives, per_device(): speed = lax.pmax(signal_speed(patch_fluid), ('fft', 'grp'))  72.9 us
    gather x1, local copies, waits for them, and re-layouts, per_device(): blocks = framed.reshape(-1)[start[None, :] + offsets[:, None]]  71.2 us
    unnamed x28, other arithmetic  29.8 us
    dot_general x2, matrix products, per_device(): columns = jnp.einsum('ky,xyz->xkz', table_y, columns, precision=HIGH)  27.5 us
    dot_general x2, matrix products, per_device(): lines = jnp.einsum('kx,xyz->kyz', table_x, lines, precision=HIGH)  26.1 us
    all_to_all x1, waiting for transfers between devices, per_device(): lax.all_to_all(lines, 'fft', split_axis=0, concat_axis=1, tiled=True)  24.2 us
    select_n x16, other arithmetic, relax(): inner = jnp.where((parity == colour)[..., None], moved, inner)  19.9 us
    all_to_all x1, waiting for transfers between devices, per_device(): spec = lax.all_to_all(lines, 'fft', split_axis=0, concat_axis=1, tiled=True)  17.3 us
  transfers between devices with their start and end apart: 12, of which 9 were waited for; matrix products, arithmetic and copies ran while one was open for 29% of the time, Pallas kernels for 0%

commit v1 on v0

v1 whole, which is shorter than its diff:
```python
import functools

import jax
import jax.numpy as jnp
import ml_dtypes
import numpy as np
from jax import lax
from jax.experimental import pallas as pl
from jax.experimental.pallas import tpu as pltpu
from jax.sharding import PartitionSpec as P

SWEEPS = 8
GAMMA = 5.0 / 3.0
SCREEN = 0.0006
OMEGA = 1.5
COURANT = 0.4
FINE_STEP = 0.5
F32 = jnp.float32
BF16 = jnp.bfloat16


def sine(count):
    index = np.arange(1, count + 1)
    return np.sqrt(2.0 / (count + 1)) * np.sin(
        np.pi * (np.outer(index, index) % (2 * (count + 1))) / (count + 1)
    )


def eigen(count):
    return 4.0 * np.sin(np.pi * np.arange(1, count + 1) / (2 * (count + 1))) ** 2


def halves(table):
    high = table.astype(ml_dtypes.bfloat16)
    low = (table - high.astype(np.float64)).astype(ml_dtypes.bfloat16)
    return np.stack([high, low])


@functools.lru_cache(None)
def tables(nf, ng, cx, cy, nz):
    ny = ng * cy
    kz = nz // ng
    sz, sy, sx, full = sine(nz), sine(cy), sine(cx), sine(ny)
    lam = eigen(cy)[:, None] + eigen(nz)[None, :] + SCREEN
    steps = [1.0 / (2.0 + lam)]
    for _ in range(1, cx // 2):
        steps.append(1.0 / (2.0 + lam - steps[-1]))
    steps.append(1.0 / (1.0 - steps[-1] ** 2))
    edge = np.zeros((ng, 2, ny))
    wide = np.zeros((ng, 128, ny))
    back = np.zeros((ng, 128, ny))
    for d in range(ng):
        if d > 0:
            edge[d, 0] = full[d * cy - 1]
        if d < ng - 1:
            edge[d, 1] = full[(d + 1) * cy]
        wide[d, :cy] = sy @ full[d * cy : (d + 1) * cy]
        back[d, :cy] = wide[d, :cy]
        back[d, cy + cx] = edge[d, 0]
        back[d, cy + cx + 1] = edge[d, 1]
    repeated = np.repeat(edge.reshape(2 * ng, ny), kz, axis=0)
    denom = (
        eigen(cx)[None, :, None, None]
        + eigen(nz).reshape(ng, 1, kz, 1)
        + eigen(ny)[None, None, None, :]
        + SCREEN
    )
    phi = 2.0 * np.arcsinh(np.sqrt(eigen(ny)[None, :] + eigen(nz)[:, None] + SCREEN) / 2.0)

    def ratio(m, n):
        return np.exp(-(n - m) * phi) * np.expm1(-2 * m * phi) / np.expm1(-2 * n * phi)

    pair = np.zeros((ng, nf, 2, 8, 128))
    for i, values in enumerate((ratio(cx - 1, cx), ratio(1, cx))):
        pair[:, :, i, :3] = values.reshape(ng, nf, 3, 128)
    spread = np.zeros((10, 6))
    for j in range(10):
        at = j / 2 + 0.25
        low = int(np.floor(at))
        spread[j, low] += 1 - (at - low)
        spread[j, low + 1] += at - low
    inner = np.zeros((8, 8))
    inner[:, :6] = spread[1:9]
    outer = np.zeros((8, 8))
    outer[0, :6] = spread[0]
    outer[7, :6] = spread[9]
    weave = np.concatenate([np.kron(np.eye(16), inner), np.kron(np.eye(16), outer)])
    lanes = np.arange(128)
    fold = ((lanes[:, None] + 1) % 8 == lanes[None, :] % 8).astype(np.float64)
    column = np.broadcast_to(sy[0][:, None], (cy, 128))
    as32 = lambda t: np.ascontiguousarray(t, dtype=np.float32)
    szh, szl = halves(sz)
    return dict(
        sz=np.block([[szh, szl], [szh, np.zeros_like(szh)]]).astype(ml_dtypes.bfloat16),
        sy=halves(sy),
        sx=as32(sx),
        steps=as32(np.stack(steps)),
        wide=halves(wide.reshape(ng * 128, ny)),
        back=halves(np.ascontiguousarray(back.reshape(ng * 128, ny).T)),
        edge=halves(repeated),
        edget=halves(np.ascontiguousarray(repeated.T)),
        inv=as32(1.0 / denom),
        pair=as32(pair),
        weave=weave.astype(ml_dtypes.bfloat16),
        fold=np.concatenate([fold, fold]).astype(ml_dtypes.bfloat16),
        column=as32(column),
    )


NAMES = (
    "sz", "sy", "sx", "steps", "wide", "back", "edge", "edget", "inv", "pair", "weave", "fold", "column",
)


def split(value):
    high = value.astype(BF16)
    return high, (value - high.astype(F32)).astype(BF16)


def mm(a, b):
    return jnp.dot(a, b, preferred_element_type=F32)


def dot_right(value, high, low):
    a, b = split(value)
    return mm(a, high) + (mm(b, high) + mm(a, low))


def dot_left(high, low, value):
    a, b = split(value)
    return mm(high, a) + (mm(high, b) + mm(low, a))


def root_kernel(
    cfg,
    ghost, rho, speed, fluid, change,
    sz_h, sy_h, sx_h, steps_h, wide_h, back_h, edge_h, edget_h, inv_h, pair_h, weave_h, fold_h, column_h,
    pot_h, fine, moved,
    src, sz, sy, sx, steps, wide, back, edge, edget, inv, pair, weave, fold, column,
    block, solved, part, grid, hfield,
    s1, r1, s2, r2, s3, r3, s4, r4, s6, r6, chain, mults, field, ghosts, force,
    tsem, osem, s1s, r1s, s2s, r2s, s3s, r3s, s4s, r4s, s6s, r6s,
):
    nf, ng, cx, cy, nz = cfg
    kz = nz // ng
    ny = ng * cy
    half = cx // 2
    f = lax.axis_index("fft")
    g = lax.axis_index("grp")

    barrier = pltpu.get_barrier_semaphore()

    def hello(axis, pos, count):
        def body(k, _):
            pl.semaphore_signal(
                barrier, inc=1, device_id={axis: lax.rem(pos + k, count)},
                device_id_type=pl.DeviceIdType.MESH,
            )
            return 0
        lax.fori_loop(1, count, body, 0)

    hello("grp", g, ng)
    hello("fft", f, nf)

    loads = {}
    order = [
        ("rho", rho, src), ("sz", sz_h, sz), ("sy", sy_h, sy), ("steps", steps_h, steps),
        ("column", column_h, column), ("pair", pair_h.at[g, f], pair), ("wide", wide_h, wide),
        ("sx", sx_h, sx), ("edge", edge_h, edge), ("inv", inv_h.at[g], inv),
        ("edget", edget_h, edget), ("back", back_h, back), ("fold", fold_h, fold), ("weave", weave_h, weave),
    ]
    for i, (name, a, b) in enumerate(order):
        loads[name] = pltpu.make_async_copy(a, b, tsem.at[i])
        loads[name].start()

    sub = lax.broadcasted_iota(jnp.int32, (8, 128), 0)
    even = lax.rem(sub, 2) == 0

    loads["rho"].wait()
    loads["sz"].wait()
    loads["sy"].wait()

    def forward(i, _):
        rows = src[pl.ds(2 * i, 2)].reshape(2 * cy, nz)
        a, b = split(rows)
        both = mm(jnp.concatenate([a, b], axis=1), sz[...])
        both = both[:, :nz] + both[:, nz:]
        pair_x = jnp.concatenate([both[:cy], both[cy:]], axis=1)
        out = dot_left(sy[0], sy[1], pair_x)
        block[2 * i] = out[:, :nz]
        block[2 * i + 1] = out[:, nz:]
        return 0

    lax.fori_loop(0, half, forward, 0)

    loads["steps"].wait()
    loads["column"].wait()

    def solve(fetch, i):
        at = pl.ds(pl.multiple_of(16 * i, 16), 16)
        low, high = [], []
        for j in range(half):
            m = steps[j, at, :]
            a, b = fetch(j, at), fetch(cx - 1 - j, at)
            if j == 0:
                low.append(-m * a)
                high.append(-m * b)
            else:
                low.append(m * (low[-1] - a))
                high.append(m * (high[-1] - b))
        m, scale = steps[half - 1, at, :], steps[half, at, :]
        a, b = low[-1], high[-1]
        low[-1] = (a + m * b) * scale
        high[-1] = (b + m * a) * scale
        for j in range(half - 2, -1, -1):
            m = steps[j, at, :]
            low[j] = low[j] + m * low[j + 1]
            high[j] = high[j] + m * high[j + 1]
        return at, low + high[::-1]

    part[...] = jnp.zeros_like(part)

    def first(i, _):
        at, values = solve(lambda x, at: block[x, at, :], i)
        col = column[at, :]
        for x in range(cx):
            v = values[x] * col
            part[x] += v[:8] + v[8:]
        solved[0, at, :] = values[0]
        solved[1, at, :] = values[cx - 1]
        return 0

    lax.fori_loop(0, cy // 16, first, 0)
    sums = part[...]
    sign = jnp.where(even, 1.0, -1.0)
    edges = (jnp.sum(sums, axis=1), jnp.sum(sums * sign[None], axis=1))
    for e in range(2):
        solved[e, pl.ds(cy, cx), :] = edges[e]
        solved[e, pl.ds(cy + cx, 8), :] = speed[...]
        s1[e] = solved[e].T

    pl.semaphore_wait(barrier, ng + nf - 2)

    def send(axis, pos, count, source, target, sends, recvs):
        def body(k, _):
            to = lax.rem(pos + k, count)
            pltpu.make_async_remote_copy(
                source(to), target(pos), sends.at[k], recvs.at[k], device_id={axis: to},
                device_id_type=pl.DeviceIdType.MESH,
            ).start()
            return 0
        lax.fori_loop(1, count, body, 0)

    def receive(axis, pos, count, source, target, sends, recvs):
        def body(k, _):
            come = lax.rem(pos + (count - k), count)
            pltpu.make_async_remote_copy(
                source(come), target(come), sends.at[k], recvs.at[k], device_id={axis: come},
                device_id_type=pl.DeviceIdType.MESH,
            ).wait()
            return 0
        lax.fori_loop(1, count, body, 0)

    slice1 = lambda d: s1.at[:, pl.ds(pl.multiple_of(d * kz, kz), kz), :]
    ex1 = ("grp", g, ng, slice1, lambda d: r1.at[d], s1s, r1s)
    send(*ex1)
    r1[g] = s1[:, pl.ds(pl.multiple_of(g * kz, kz), kz), :]

    loads["pair"].wait()
    ca, cb = pair[0], pair[1]
    ca2, cb2 = ca * ca, cb * cb

    def coefficients(i, m):
        m0 = 1.0 / (1.0 - ca2 * m)
        mults[2 * i] = m0
        m1 = 1.0 / (1.0 - cb2 * m0)
        mults[2 * i + 1] = m1
        return m1

    lax.fori_loop(0, nf, coefficients, jnp.zeros((8, 128), F32))
    loads["wide"].wait()
    loads["sx"].wait()
    loads["edge"].wait()
    loads["inv"].wait()
    receive(*ex1)

    main = jnp.concatenate([r1[d].reshape(2 * kz, 128) for d in range(ng)], axis=1)
    main = dot_right(main, wide[0], wide[1])
    across = r1[...].reshape(ng * 2 * kz, 128).T
    edge_x = across[cy : cy + cx]
    most = across[cy + cx : cy + cx + 8]
    most = jnp.max(jnp.maximum(most[:, :128], most[:, 128:]), axis=0, keepdims=True)
    edge_k = jnp.dot(sx[...], edge_x, precision=lax.Precision.HIGHEST, preferred_element_type=F32)
    wide_lane = ng * 2 * kz
    diag = (
        lax.rem(lax.broadcasted_iota(jnp.int32, (kz, wide_lane), 1), kz)
        == lax.broadcasted_iota(jnp.int32, (kz, wide_lane), 0)
    )
    zero = jnp.zeros((kz, wide_lane), F32)
    sums = [jnp.zeros((kz, ny), F32), jnp.zeros((kz, ny), F32)]
    first_row = [float(v) for v in sine(cx)[0]]
    group = 4
    for x0 in range(0, cx, group):
        lhs = jnp.concatenate(
            [jnp.where(diag, jnp.broadcast_to(edge_k[x : x + 1], (kz, wide_lane)), zero) for x in range(x0, x0 + group)],
            axis=0,
        )
        out = dot_right(lhs, edge[0], edge[1])
        for x in range(x0, x0 + group):
            hd = out[(x - x0) * kz : (x - x0 + 1) * kz] * inv[x]
            hfield[x] = hd
            sums[x % 2] = sums[x % 2] + first_row[x] * hd
    rows = (main[:kz] + (sums[0] + sums[1]), main[kz:] + (sums[0] - sums[1]))
    for row in range(2):
        for j in range(6):
            s2[pl.ds((j // 3) * 8 + row * 3 + j % 3, kz, stride=16), :] = rows[row][:, j * 128 : (j + 1) * 128]
    for r in (6, 7):
        s2[pl.ds(r, nf, stride=8), :] = jnp.broadcast_to(most, (nf, 128))

    tile = lambda ref: lambda d: ref.at[pl.ds(pl.multiple_of(d * 8, 8), 8), :]
    ex2 = ("fft", f, nf, tile(s2), tile(r2), s2s, r2s)
    send(*ex2)
    mine = pl.ds(pl.multiple_of(f * 8, 8), 8)
    r2[mine, :] = s2[mine, :]
    receive(*ex2)
    most = jnp.max(r2[pl.ds(6, nf, stride=8), :])
    step = COURANT * FINE_STEP / most

    last = jnp.zeros((8, 128), F32)
    prev = last
    for d in range(nf):
        msg = r2[8 * d : 8 * d + 8, :]
        other = pltpu.roll(msg, 5, 0)
        m0, m1 = mults[2 * d], mults[2 * d + 1]
        prev = m0 * (msg - cb * other) + (m0 * ca) * prev
        chain[2 * d] = prev
        prev = m1 * (other - cb * msg) + (m1 * cb) * prev
        chain[2 * d + 1] = prev
    chain[2 * nf - 1] = prev
    for j in range(2 * nf - 2, -1, -1):
        prev = chain[j] + (mults[j] * (cb if j % 2 == 0 else ca)) * prev
        chain[j] = prev
    for d in range(nf):
        left = chain[2 * d - 1] if d > 0 else last
        right = chain[2 * d + 2] if d < nf - 1 else last
        s3[8 * d : 8 * d + 8, :] = jnp.where(sub < 3, left, pltpu.roll(right, 3, 0))

    ex3 = ("fft", f, nf, tile(s3), tile(r3), s3s, r3s)
    send(*ex3)
    r3[mine, :] = s3[mine, :]
    loads["edget"].wait()
    loads["back"].wait()
    receive(*ex3)
    around = [
        jnp.concatenate(
            [r3[pl.ds((j // 3) * 8 + row * 3 + j % 3, kz, stride=16), :] for j in range(6)], axis=1
        )
        for row in range(2)
    ]
    out_rows = dot_right(jnp.concatenate(around, axis=0), back[0], back[1])
    mixed = (around[0] + around[1], around[0] - around[1])
    corr = []
    for x0 in range(0, cx, group):
        lhs = jnp.concatenate(
            [hfield[x] + (first_row[x] * inv[x]) * mixed[x % 2] for x in range(x0, x0 + group)], axis=0
        )
        out = dot_right(lhs, edget[0], edget[1])
        for x in range(group):
            corr.append(jnp.sum(jnp.where(diag, out[x * kz : (x + 1) * kz], zero), axis=0, keepdims=True))
    corr = jnp.concatenate(corr, axis=0)
    corr = jnp.dot(sx[...], corr, precision=lax.Precision.HIGHEST, preferred_element_type=F32)
    blank = jnp.zeros((cx, kz), F32)
    from_left = jnp.concatenate([blank, edge_x[:, :-kz]], axis=1)
    from_right = jnp.concatenate([edge_x[:, kz:], blank], axis=1)
    second = lax.rem(lax.broadcasted_iota(jnp.int32, (cx, wide_lane), 1) // kz, 2) == 1
    sides = corr + jnp.where(second, from_right, from_left)
    sides = jnp.concatenate(
        [jnp.zeros((cy, wide_lane), F32), sides, jnp.zeros((128 - cy - cx, wide_lane), F32)], axis=0
    ).T
    for d in range(ng):
        s4[d] = (out_rows[:, 128 * d : 128 * d + 128] + sides[2 * kz * d : 2 * kz * (d + 1)]).reshape(2, kz, 128)

    ex4 = ("grp", g, ng, lambda d: s4.at[d], lambda d: r4.at[:, d], s4s, r4s)
    send(*ex4)
    r4[:, g] = s4[g]
    receive(*ex4)
    for e in range(2):
        solved[e] = r4[e].reshape(nz, 128).T

    def second_solve(i, _):
        def fetch(x, at):
            va = solved[0, pl.ds(cy + x, 1), :]
            vb = solved[1, pl.ds(cy + x, 1), :]
            w = jnp.where(even, va + vb, va - vb)
            value = block[x, at, :] - column[at, :] * jnp.concatenate([w, w], axis=0)
            if x == 0:
                value = value - solved[0, at, :]
            if x == cx - 1:
                value = value - solved[1, at, :]
            return value

        at, values = solve(fetch, i)
        for x in range(cx):
            block[x, at, :] = values[x]
        return 0

    lax.fori_loop(0, cy // 16, second_solve, 0)

    def inverse_z(rows):
        a, b = split(rows)
        both = mm(jnp.concatenate([a, b], axis=1), sz[...])
        return both[:, :nz] + both[:, nz:]

    def backward(i, _):
        pair_x = jnp.concatenate([block[2 * i], block[2 * i + 1]], axis=1)
        out = dot_left(sy[0], sy[1], pair_x)
        out = inverse_z(jnp.concatenate([out[:, :nz], out[:, nz:]], axis=0))
        grid[2 * i + 1, pl.ds(8, cy), :] = out[:cy]
        grid[2 * i + 2, pl.ds(8, cy), :] = out[cy:]
        return 0

    lax.fori_loop(0, half, backward, 0)
    copy_out = pltpu.make_async_copy(grid.at[pl.ds(1, cx), pl.ds(8, cy), :], pot_h, osem)
    copy_out.start()
    pair_x = jnp.concatenate([solved[0, :cy], solved[1, :cy]], axis=1)
    out = dot_left(sy[0], sy[1], pair_x)
    rest = jnp.concatenate([out[:, :nz], out[:, nz:], solved[0, cy:], solved[1, cy:]], axis=0)
    rest = inverse_z(rest)
    grid[0, pl.ds(8, cy), :] = rest[:cy]
    grid[cx + 1, pl.ds(8, cy), :] = rest[cy : 2 * cy]
    pad = 128 - cy
    for e in range(2):
        lines = rest[2 * cy + pad * e : 2 * cy + pad * (e + 1)]
        at = pl.ds(7 if e == 0 else 8 + cy, 1)
        for x in range(cx):
            grid[x + 1, at, :] = lines[x : x + 1]
    for e in range(2):
        lines = rest[2 * cy + pad * e : 2 * cy + pad * (e + 1)]
        for s in range(2):
            grid[(cx + 1) * e, pl.ds(7 if s == 0 else 8 + cy, 1), :] = lines[cx + s : cx + s + 1]

    loads["fold"].wait()
    loads["weave"].wait()
    per_y, per_z = cy // 4, nz // 4
    lanes8 = lax.broadcasted_iota(jnp.int32, (8, 128), 1)
    pick = (
        lax.broadcasted_iota(jnp.int32, (16, 128), 1) // 8 == lax.broadcasted_iota(jnp.int32, (16, 128), 0)
    )
    lane6 = lax.rem(lax.broadcasted_iota(jnp.int32, (6, 128), 1), 8)
    row6 = lax.broadcasted_iota(jnp.int32, (6, 128), 0)
    some = 4

    def gather(i, _):
        cut, odd = [], []
        for c in range(2 * some):
            code = jnp.maximum(ghost[0, 2 * some * i + c], 0)
            ix = code // (per_y * per_z)
            iy = lax.rem(code // per_z, per_y)
            iz = lax.rem(code, per_z)
            rows = grid[pl.ds(4 * ix, 6), pl.ds(7 + 4 * iy, 8), :]
            inside = (lanes8 >= 4 * iz - 1) & (lanes8 <= 4 * iz + 4) & (sub < 6)
            cut.append(jnp.where(inside[None], rows, 0.0).reshape(48, 128))
            odd.append(lax.rem(iz, 2))
        a, b = split(jnp.concatenate(cut, axis=0))
        out = mm(jnp.concatenate([a, b], axis=1), fold[...]).reshape(2 * some * 3, 16, 128)
        out = jnp.sum(jnp.where(pick[None], out, 0.0), axis=1)
        for k in range(some):
            d = some * i + k
            mini = out[6 * k : 6 * k + 6]
            turned = jnp.where(lane6 < 4, pltpu.roll(mini, 124, 1), pltpu.roll(mini, 4, 1))
            which = jnp.where(row6 < 3, odd[2 * k], odd[2 * k + 1])
            mini = jnp.where(which == 1, turned, mini)
            slots = [
                jnp.full((1, 128), ghost[1, 2 * d + c].astype(F32), F32) for c in range(2)
            ]
            s6[pl.ds(pl.multiple_of(8 * d, 8), 8), :] = jnp.concatenate([mini] + slots, axis=0)
        return 0

    lax.fori_loop(0, nf // some, gather, 0)

    ex6 = ("fft", f, nf, tile(s6), tile(r6), s6s, r6s)
    send(*ex6)
    r6[mine, :] = s6[mine, :]
    receive(*ex6)
    lanes = lax.broadcasted_iota(jnp.int32, (nf, 128), 1)
    hot = jnp.concatenate(
        [
            jnp.where(r6[pl.ds(6 + c, nf, stride=8), :] == lanes.astype(F32), 1.0, 0.0)
            for c in range(2)
        ],
        axis=0,
    ).astype(BF16)
    within, outside = [], []
    for t in range(3):
        came = jnp.concatenate([r6[pl.ds(c * 3 + t, nf, stride=8), :] for c in range(2)], axis=0)
        a, b = split(came.T)
        placed = mm(a, hot) + mm(b, hot)
        a, b = split(placed)
        woven = mm(weave[...], a) + mm(weave[...], b)
        woven = woven.reshape(2, 2, 8, 8, 128)[..., : fine.shape[-1]]
        within += [woven[0, 0], woven[0, 1]]
        outside += [woven[1, 0], woven[1, 1]]

    def between(values, j):
        low = j // 2
        return (
            0.75 * values[low] + 0.25 * values[low + 1]
            if j % 2 == 0
            else 0.25 * values[low] + 0.75 * values[low + 1]
        )

    scale = 1.0 / (6.0 + SCREEN * FINE_STEP * FINE_STEP)
    for jx in range(10):
        plane = between(within, jx)
        for jy in range(10):
            field[jx, jy] = between(plane, jy)
        if 1 <= jx <= 8:
            plane = between(outside, jx)
            for jy in range(1, 9):
                layer = between(plane, jy)
                ghosts[jx - 1, jy - 1] = layer
                force[jx - 1, jy - 1] = (OMEGA * scale) * (
                    layer - FINE_STEP * FINE_STEP * fluid[0, jx - 1, jy - 1]
                )

    width = fine.shape[-1]
    z = lax.broadcasted_iota(jnp.int32, (8, width), 0)
    bottom, top, zeven = z == 0, z == 7, lax.rem(z, 2) == 0
    zodd = jnp.logical_not(zeven)

    def sweep(_, carry):
        for colour in (0, 1):
            def planes(i, c, colour=colour):
                for k in range(2):
                    x = 2 * i + k + 1
                    for y in range(1, 9):
                        v = field[x, y]
                        near = (
                            (field[x - 1, y] + field[x + 1, y])
                            + (field[x, y - 1] + field[x, y + 1])
                            + (
                                jnp.where(bottom, 0.0, pltpu.roll(v, 1, 0))
                                + jnp.where(top, 0.0, pltpu.roll(v, 7, 0))
                            )
                        )
                        new = (1.0 - OMEGA) * v + ((OMEGA * scale) * near + force[x - 1, y - 1])
                        mask = zeven if (k + y - 1 + colour) % 2 == 0 else zodd
                        field[x, y] = jnp.where(mask, new, v)
                return c
            lax.fori_loop(0, 4, planes, 0)
        return carry

    lax.fori_loop(0, SWEEPS, sweep, 0)

    def update(x, _):
        for y in range(8):
            v = field[x + 1, y + 1]
            layer = ghosts[x, y]
            fine[x, y] = v
            pull = (
                field[x, y + 1] - field[x + 2, y + 1],
                field[x + 1, y] - field[x + 1, y + 2],
                jnp.where(bottom, layer, pltpu.roll(v, 1, 0)) - jnp.where(top, layer, pltpu.roll(v, 7, 0)),
            )
            dens = fluid[0, x, y]
            rate = step / FINE_STEP
            work = 0.0
            moved[0, x, y] = dens - rate * change[0, x, y]
            for n in range(3):
                mom = fluid[1 + n, x, y]
                moved[1 + n, x, y] = mom - rate * change[1 + n, x, y] + step * dens * pull[n]
                work = work + mom * pull[n]
            moved[4, x, y] = fluid[4, x, y] - rate * change[4, x, y] + step * work
        return 0

    lax.fori_loop(0, 8, update, 0)
    copy_out.wait()


def root_call(ghost, rho, speed, fluid, change, nf, ng):
    cx, cy, nz = rho.shape
    kz = nz // ng
    ny = ng * cy
    count = fluid.shape[-1]
    tab = tables(nf, ng, cx, cy, nz)
    consts = [jnp.asarray(tab[n]) for n in NAMES]
    vm = lambda shape, dtype=F32: pltpu.VMEM(shape, dtype)
    anyspace = pl.BlockSpec(memory_space=pl.ANY)
    vspace = pl.BlockSpec(memory_space=pltpu.VMEM)
    dma = pltpu.SemaphoreType.DMA
    local = {n: tab[n].shape for n in NAMES}
    local["inv"] = local["inv"][1:]
    local["pair"] = local["pair"][2:]
    return pl.pallas_call(
        functools.partial(root_kernel, (nf, ng, cx, cy, nz)),
        out_shape=(
            jax.ShapeDtypeStruct((cx, cy, nz), F32),
            jax.ShapeDtypeStruct((8, 8, 8, count), F32),
            jax.ShapeDtypeStruct((5, 8, 8, 8, count), F32),
        ),
        in_specs=[pl.BlockSpec(memory_space=pltpu.SMEM), anyspace, vspace, vspace, vspace]
        + [anyspace] * len(NAMES),
        out_specs=(anyspace, vspace, vspace),
        scratch_shapes=[vm((cx, cy, nz))]
        + [vm(local[n], consts[i].dtype) for i, n in enumerate(NAMES)]
        + [
            vm((cx, cy, nz)),
            vm((2, 128, nz)),
            vm((cx, 8, nz)),
            vm((cx + 2, cy + 16, nz)),
            vm((cx, kz, ny)),
            vm((2, nz, 128)), vm((ng, 2, kz, 128)),
            vm((nf * 8, 128)), vm((nf * 8, 128)),
            vm((nf * 8, 128)), vm((nf * 8, 128)),
            vm((ng, 2, kz, 128)), vm((2, ng, kz, 128)),
            vm((nf * 8, 128)), vm((nf * 8, 128)),
            vm((2 * nf, 8, 128)), vm((2 * nf, 8, 128)),
            vm((10, 10, 8, count)), vm((8, 8, 8, count)), vm((8, 8, 8, count)),
            dma((14,)), dma,
            dma((ng,)), dma((ng,)),
            dma((nf,)), dma((nf,)),
            dma((nf,)), dma((nf,)),
            dma((ng,)), dma((ng,)),
            dma((nf,)), dma((nf,)),
        ],
        compiler_params=pltpu.CompilerParams(
            collective_id=0, has_side_effects=True, vmem_limit_bytes=56 * 1024 * 1024
        ),
    )(ghost, rho, speed, fluid, change, *consts)


def primitives(fluid):
    dens = fluid[0]
    vel = fluid[1:4] / dens
    kinetic = 0.5 * jnp.sum(fluid[1:4] * vel, axis=0)
    pres = (GAMMA - 1.0) * (fluid[4] - kinetic)
    return (dens, vel, pres)


def signal_speed(fluid):
    dens, vel, pres = primitives(fluid[:, 2:10, 2:10, 2:10])
    sound = jnp.sqrt(GAMMA * pres / dens)
    return jnp.max(jnp.max(jnp.abs(vel), axis=0) + sound)


def along(array, axis, start, stop):
    return lax.slice_in_dim(array, start, stop, axis=axis + 1)


def conserved_flux(state, axis):
    dens = state[0]
    vel = state[1:4]
    pres = state[4]
    normal = vel[axis]
    energy = pres / (GAMMA - 1.0) + 0.5 * dens * jnp.sum(vel * vel, axis=0)
    cons = jnp.stack([dens, dens * vel[0], dens * vel[1], dens * vel[2], energy])
    moment = [dens * normal * vel[other] + (pres if other == axis else 0.0) for other in range(3)]
    flux = jnp.stack([dens * normal, moment[0], moment[1], moment[2], (energy + pres) * normal])
    speed = jnp.abs(normal) + jnp.sqrt(GAMMA * pres / dens)
    return (cons, flux, speed)


def flux_difference(prim, axis):
    for other in range(3):
        if other != axis:
            prim = along(prim, other, 2, 10)
    left_diff = along(prim, axis, 1, 11) - along(prim, axis, 0, 10)
    right_diff = along(prim, axis, 2, 12) - along(prim, axis, 1, 11)
    slope = (
        0.5
        * (jnp.sign(left_diff) + jnp.sign(right_diff))
        * jnp.minimum(jnp.abs(left_diff), jnp.abs(right_diff))
    )
    centre = along(prim, axis, 1, 11)
    upper = centre + 0.5 * slope
    lower = centre - 0.5 * slope
    cons_left, flux_left, speed_left = conserved_flux(along(upper, axis, 0, 9), axis)
    cons_right, flux_right, speed_right = conserved_flux(along(lower, axis, 1, 10), axis)
    flux = 0.5 * (flux_left + flux_right) - 0.5 * jnp.maximum(speed_left, speed_right) * (
        cons_right - cons_left
    )
    return along(flux, axis, 1, 9) - along(flux, axis, 0, 8)


def per_device(root_density, patch_fluid, ghost_list):
    nf = lax.axis_size("fft")
    ng = lax.axis_size("grp")
    speed = jnp.broadcast_to(signal_speed(patch_fluid), (8, 128))
    dens, vel, pres = primitives(patch_fluid)
    prim = jnp.concatenate([dens[None], vel, pres[None]], axis=0)
    change = flux_difference(prim, 0) + flux_difference(prim, 1) + flux_difference(prim, 2)
    inner = patch_fluid[:, 2:10, 2:10, 2:10]
    return root_call(ghost_list[:, 0], root_density, speed, inner, change, nf, ng)


def solution(mesh):
    return jax.shard_map(
        per_device,
        mesh=mesh,
        in_specs=(
            P("fft", "grp", None),
            P(None, None, None, None, ("fft", "grp")),
            P(None, ("fft", "grp"), None),
        ),
        out_specs=(
            P("fft", "grp", None),
            P(None, None, None, ("fft", "grp")),
            P(None, None, None, None, ("fft", "grp")),
        ),
        check_vma=False,
    )
```

time: 545 us -> 97.7 us (0.18)
  local copies, waits for them, and re-layouts: 124 us -> 8.51 us
  waiting for transfers between devices: 105 us -> 0 us
  other arithmetic: 99.6 us -> 19.3 us
  starting transfers between devices: 77.6 us -> 0 us
  blocking collectives: 72.9 us -> 0 us
  Pallas kernels: 0 us -> 68.7 us
  matrix products: 58.6 us -> 0 us
    all_to_all x8 -> x0, waiting for transfers between devices: 97.7 us -> none  [the longest x1 24.2 us: per_device(): lax.all_to_all(lines, 'fft', split_axis=0, concat_axis=1, tiled=True)]
    pmax x1 -> x0, blocking collectives: 72.9 us -> none  [per_device(): speed = lax.pmax(signal_speed(patch_fluid), ('fft', 'grp'))]
    gather x1 -> x0, local copies, waits for them, and re-layouts: 71.2 us -> none  [per_device(): blocks = framed.reshape(-1)[start[None, :] + offsets[:, None]]]
    pallas_call x0 -> x1, Pallas kernels: none -> 68.7 us  [root_call(): pl.pallas_call(functools.partial(root_kernel, (nf, ng, cx, cy, nz)), out_...]
    all_to_all x8 -> x0, starting transfers between devices: 65 us -> none  [the longest x1 12.5 us: per_device(): lines = lax.all_to_all(spec, 'fft', split_axis=1, concat_axis=0, tiled=True)]
    dot_general x10 -> x0, matrix products: 58.6 us -> none  [the longest x2 27.5 us: per_device(): columns = jnp.einsum('ky,xyz->xkz', table_y, columns, precision=HIGH)]
    unnamed x28, other arithmetic: 29.8 us -> 2.33 us
    select_n x17 -> x0, other arithmetic: 20.7 us -> none  [the longest x16 19.9 us: relax(): inner = jnp.where((parity == colour)[..., None], moved, inner)]
  transfers between devices with their start and end apart: 12 -> 0, of which waited for: 9 -> 0; matrix products, arithmetic and copies ran while one was open for 29% -> 0% of each run, Pallas kernels for 0% -> 0%
where the time goes in v1:
time: 97.7 us; the launch traced here: 97.5 us
  Pallas kernels  68.7 us (70%)
  other arithmetic  19.3 us (20%)
  local copies, waits for them, and re-layouts  8.51 us (9%)
  between operations  1.05 us (1%)
    pallas_call x1, Pallas kernels, root_call(): pl.pallas_call(functools.partial(root_kernel, (nf, ng, cx, cy, nz)), out_...  68.7 us
    add x3, other arithmetic, flux_difference(): upper = centre + 0.5 * slope  5.12 us
    unnamed x17, local copies, waits for them, and re-layouts  4.43 us
    reduce_sum x2, other arithmetic, primitives(): kinetic = 0.5 * jnp.sum(fluid[1:4] * vel, axis=0)  3.26 us
    unnamed x28, other arithmetic  2.33 us
    sub x3, other arithmetic, flux_difference(): 0.5 * (flux_left + flux_right)  2.3 us

profile of v1, /device:TPU:1, one launch (start us, length us, event | category | flops | bytes accessed | tf_op | source)
XLA Modules:
  0.0 97.5 jit_solution(9392054494279807129)
XLA Ops:
  0.6 1.6 %fusion.26 = (f32[1,12,12,12,32]{4,3,2,1,0:T(8,128)S(1)}, f32[12,12,12,32]{3,2,1,0:T(8,128)S(1)}) fusion(f32[5,12,12,12,32]{4,3,2,1,0:T(8,128)} %param.17), kind=kLoop, calls=%fused_computation.135 | loop fusion | bytes 663552 | tf_op jit(solution)/shard_map/slice | solution.py:633
  2.2 3.0 %multiply_reduce_fusion = (f32[12,12,12,32]{3,2,1,0:T(8,128)S(1)}, f32[3,12,12,12,32]{4,3,2,1,0:T(8,128)S(1)}) fusion(f32[5,12,12,12,32]{4,3,2,1,0:T(8,128)} %param.17, f32[12,12,12,32]{3,2,1,0:T(8,128)S(1)} %get-tuple-element.26), kind=kLoop, calls=%fused_computation.1 | loop fusion | flops 442368 | bytes 1769472 | tf_op jit(solution)/shard_map/reduce_sum | solution.py:635
  5.3 0.3 fusion.10
  5.5 0.9 pad_maximum_fusion
  6.5 1.0 %fusion.5 = (f32[5,10,8,8,32]{4,3,2,1,0:T(8,128)S(1)}, f32[5,10,8,8,32]{4,3,2,1,0:T(8,128)S(1)}) fusion(f32[5,12,12,12,32]{4,3,2,1,0:T(8,128)S(1)} %pad_maximum_fusion), kind=kLoop, calls=%fused_computation.20 | loop fusion | flops 1331200 | bytes 2048000 | tf_op jit(solution)/shard_map/add | solution.py:675
  7.5 0.1 constant_dynamic-update-slice_fusion
  7.6 0.1 multiply_dynamic-update-slice_fusion.29
  7.7 0.1 multiply_dynamic-update-slice_fusion.28
  7.9 0.1 multiply_dynamic-update-slice_fusion.26
  8.0 0.1 multiply_dynamic-update-slice_fusion.25
  8.1 0.1 multiply_dynamic-update-slice_fusion.20
  8.2 0.2 fusion.13
  8.4 0.3 multiply_dynamic-update-slice_fusion.27
  8.8 0.1 multiply_dynamic-update-slice_fusion.24
  8.9 0.8 multiply_subtract_fusion.2
  9.7 1.6 %fusion.3 = (f32[5,8,10,8,32]{4,3,2,1,0:T(8,128)S(1)}, f32[5,8,10,8,32]{4,3,2,1,0:T(8,128)S(1)}) fusion(f32[5,12,12,12,32]{4,3,2,1,0:T(8,128)S(1)} %pad_maximum_fusion), kind=kLoop, calls=%fused_computation.16 | loop fusion | flops 1331200 | bytes 2048000 | tf_op jit(solution)/shard_map/add | solution.py:675
  11.4 0.1 add_dynamic-update-slice_fusion.2
  11.5 0.1 multiply_dynamic-update-slice_fusion.15
  11.7 0.1 add_dynamic-update-slice_fusion.3
  11.8 0.1 multiply_dynamic-update-slice_fusion.18
  11.9 0.1 multiply_dynamic-update-slice_fusion.10
  11.9 0.2 fusion.11
  12.1 0.3 multiply_dynamic-update-slice_fusion.17
  12.4 0.1 multiply_dynamic-update-slice_fusion.14
  12.5 0.3 multiply_subtract_fusion.1
  12.8 2.5 %fusion.1 = (f32[5,8,8,10,32]{4,3,2,1,0:T(8,128)S(1)}, f32[5,8,8,10,32]{4,3,2,1,0:T(8,128)S(1)}) fusion(f32[5,12,12,12,32]{4,3,2,1,0:T(8,128)S(1)} %pad_maximum_fusion), kind=kLoop, calls=%fused_computation.8 | loop fusion | flops 1331200 | bytes 2048000 | tf_op jit(solution)/shard_map/add | solution.py:675
  15.3 0.1 constant_dynamic-update-slice_fusion.12
  15.4 0.1 multiply_dynamic-update-slice_fusion.9
  15.5 0.1 multiply_dynamic-update-slice_fusion.8
  15.6 0.2 add_dynamic-update-slice_fusion.1
  15.8 0.1 constant_dynamic-update-slice_fusion.13
  16.0 0.1 multiply_dynamic-update-slice_fusion.6
  16.1 0.1 multiply_dynamic-update-slice_fusion.5
  16.2 0.3 add_dynamic-update-slice_fusion
  16.5 0.2 multiply_dynamic-update-slice_fusion
  16.7 0.7 fusion.6
  17.4 0.7 multiply_dynamic-update-slice_fusion.7
  18.1 0.2 multiply_dynamic-update-slice_fusion.4
  18.3 1.2 %multiply_subtract_fusion = f32[5,8,8,9,32]{4,3,2,1,0:T(8,128)S(1)} fusion(f32[5,8,8,9,32]{4,3,2,1,0:T(8,128)S(1)} %get-tuple-element.28, f32[5,8,8,9,32]{4,3,2,1,0:T(8,128)S(1)} %get-tuple-element.30, f32[5,8,8,9,32]{4,3,2,1,0:T(8,128)S(1)} %get-tuple-element.29, f32[5,8,8,9,32]{4,3,2,1,0:T(8,128)S(1)} %get-tuple-element.27, ...), kind=kLoop, calls=%fused_computation.5 | loop fusion | flops 460800 | bytes 1916928 | tf_op jit(solution)/shard_map/sub | solution.py:679
  19.5 1.4 %fusion.8.change = f32[5,8,8,8,32]{4,3,2,1,0:T(8,128)} fusion(f32[5,8,8,9,32]{4,3,2,1,0:T(8,128)S(1)} %multiply_subtract_fusion, f32[5,8,9,8,32]{4,3,2,1,0:T(8,128)S(1)} %multiply_subtract_fusion.1, f32[5,9,8,8,32]{4,3,2,1,0:T(8,128)S(1)} %multiply_subtract_fusion.2), kind=kLoop, calls=%fused_computation.29 | loop fusion | flops 409600 | bytes 2293760 | tf_op jit(solution)/shard_map/add | solution.py:691
  21.0 0.3 multiply_reduce_fusion.1
  21.3 0.8 fusion.25
  22.1 1.2 %broadcast_in_dim.2.speed = f32[8,128]{1,0:T(8,128)} broadcast(f32[]{:T(128)} %fusion.25), dimensions={} | broadcast | bytes 4100 | tf_op jit(solution)/shard_map/broadcast_in_dim | solution.py:688
  23.3 1.2 %slice.273.fluid = f32[5,8,8,8,32]{4,3,2,1,0:T(8,128)} slice(f32[5,12,12,12,32]{4,3,2,1,0:T(8,128)S(1)} %bitcast.78), slice={[0:5], [2:10], [2:10], [2:10], [0:32]} | slice | bytes 655360 | tf_op jit(solution)/shard_map/slice | solution.py:641
  24.5 68.7 %shard_map.175 = (f32[24,96,128]{2,1,0:T(8,128)}, f32[8,8,8,32]{3,2,1,0:T(8,128)}, f32[5,8,8,8,32]{4,3,2,1,0:T(8,128)}) custom-call(s32[2,64]{1,0:T(2,128)} %bitcast.79, f32[24,96,128]{2,1,0:T(8,128)} %rho.1, f32[8,128]{1,0:T(8,128)} %broadcast_in_dim.2.speed, f32[5,8,8,8,32]{4,3,2,1,0:T(8,128)} %slice.273.fluid, f32[5,8,8,8,32]{4,3,2,1,0:T(8,128)} %fusion.8.change, ...), custom_call_target="tpu_custom_call" | custom-call | tf_op jit(solution)/shard_map/pallas_call | solution.py:594
  93.2 2.5 %copy.70 = f32[24,96,128]{2,1,0:T(8,128)} copy(f32[24,96,128]{2,1,0:T(8,128)} %get-tuple-element.81) | data formatting | bytes 2359296
  95.7 0.7 copy.71
  96.4 1.1 %copy.72 = f32[5,8,8,8,32]{4,3,2,1,0:T(8,128)} copy(f32[5,8,8,8,32]{4,3,2,1,0:T(8,128)S(1)} %copy-done) | data formatting | bytes 655360
  (23 shorter events, 0.5 us)
Async XLA Ops:
  0.6 4.6 %slice-start = ((s8[5898240]{0:T(1024)(128)(4,1)}), s8[4194304]{0:T(1024)(128)(4,1)S(1)}, s32[]{:S(2)}) async-start(s8[5898240]{0:T(1024)(128)(4,1)} %bitcast.77), calls=%async_computation | async-start | bytes 8388608
  2.2 3.0 %slice-start.1 = ((s8[5898240]{0:T(1024)(128)(4,1)}), s8[1703936]{0:T(1024)(128)(4,1)S(1)}, s32[]{:S(2)}) async-start(s8[5898240]{0:T(1024)(128)(4,1)} %bitcast.77), calls=%async_computation.1 | async-start | bytes 3407872
  93.2 2.5 %copy-start.1 = (f32[8,8,8,32]{3,2,1,0:T(8,128)S(1)}, f32[8,8,8,32]{3,2,1,0:T(8,128)}, u32[]{:S(2)}) copy-start(f32[8,8,8,32]{3,2,1,0:T(8,128)} %get-tuple-element.82) | copy-start | bytes 196612
  93.2 3.2 %copy-start = (f32[5,8,8,8,32]{4,3,2,1,0:T(8,128)S(1)}, f32[5,8,8,8,32]{4,3,2,1,0:T(8,128)}, u32[]{:S(2)}) copy-start(f32[5,8,8,8,32]{4,3,2,1,0:T(8,128)} %get-tuple-element.83) | copy-start | bytes 983044

commit v2 on v1

--- a/solution.py
+++ b/solution.py
@@ -108,7 +108,7 @@
 
 
 NAMES = (
-    "sz", "sy", "sx", "steps", "wide", "back", "edge", "edget", "inv", "pair", "weave", "fold", "column",
+    "sz", "sy", "sx", "steps", "wide", "back", "edge", "edget", "inv", "pair", "fold", "column",
 )
 
 
@@ -133,12 +133,12 @@
 
 def root_kernel(
     cfg,
-    ghost, rho, speed, fluid, change,
-    sz_h, sy_h, sx_h, steps_h, wide_h, back_h, edge_h, edget_h, inv_h, pair_h, weave_h, fold_h, column_h,
-    pot_h, fine, moved,
-    src, sz, sy, sx, steps, wide, back, edge, edget, inv, pair, weave, fold, column,
+    ghost, rho, fluid_h,
+    sz_h, sy_h, sx_h, steps_h, wide_h, back_h, edge_h, edget_h, inv_h, pair_h, fold_h, column_h,
+    pot_h, blocks, most_out, change,
+    src, sz, sy, sx, steps, wide, back, edge, edget, inv, pair, fold, column, fluid, prim,
     block, solved, part, grid, hfield,
-    s1, r1, s2, r2, s3, r3, s4, r4, s6, r6, chain, mults, field, ghosts, force,
+    s1, r1, s2, r2, s3, r3, s4, r4, s6, r6, chain, mults, last_face,
     tsem, osem, s1s, r1s, s2s, r2s, s3s, r3s, s4s, r4s, s6s, r6s,
 ):
     nf, ng, cx, cy, nz = cfg
@@ -148,6 +148,8 @@
     f = lax.axis_index("fft")
     g = lax.axis_index("grp")
 
+    ny_chips = 4 if nf % 4 == 0 else 1
+    nz_chips = nf // ny_chips
     barrier = pltpu.get_barrier_semaphore()
 
     def hello(axis, pos, count):
@@ -167,7 +169,7 @@
         ("rho", rho, src), ("sz", sz_h, sz), ("sy", sy_h, sy), ("steps", steps_h, steps),
         ("column", column_h, column), ("pair", pair_h.at[g, f], pair), ("wide", wide_h, wide),
         ("sx", sx_h, sx), ("edge", edge_h, edge), ("inv", inv_h.at[g], inv),
-        ("edget", edget_h, edget), ("back", back_h, back), ("fold", fold_h, fold), ("weave", weave_h, weave),
+        ("fluid", fluid_h, fluid), ("edget", edget_h, edget), ("back", back_h, back), ("fold", fold_h, fold),
     ]
     for i, (name, a, b) in enumerate(order):
         loads[name] = pltpu.make_async_copy(a, b, tsem.at[i])
@@ -236,33 +238,182 @@
     edges = (jnp.sum(sums, axis=1), jnp.sum(sums * sign[None], axis=1))
     for e in range(2):
         solved[e, pl.ds(cy, cx), :] = edges[e]
-        solved[e, pl.ds(cy + cx, 8), :] = speed[...]
+        solved[e, pl.ds(cy + cx, 8), :] = jnp.zeros((8, 128), F32)
         s1[e] = solved[e].T
 
+
+    cells = pl.ds(2, 8)
+
+    def cell_values(cons):
+        dens = cons[0]
+        over = 1.0 / dens
+        vel = [m * over for m in cons[1:4]]
+        kinetic = 0.5 * (cons[1] * vel[0] + cons[2] * vel[1] + cons[3] * vel[2])
+        return [dens] + vel + [(GAMMA - 1.0) * (cons[4] - kinetic)]
+
+    def sound(dens, pres):
+        return jnp.sqrt(GAMMA * pres) * lax.rsqrt(dens)
+
+    def make_cells(x, _):
+        for y in range(12):
+            w = cell_values([fluid[v, x, y, cells, :] for v in range(5)])
+            for v in range(5):
+                prim[v, x, y] = w[v]
+        return 0
+
+    def top_speed():
+        def body(x, top):
+            for y in range(2, 10):
+                w = [prim[v, x + 2, y] for v in range(5)]
+                fast = jnp.maximum(jnp.maximum(jnp.abs(w[1]), jnp.abs(w[2])), jnp.abs(w[3]))
+                top = jnp.maximum(top, fast + sound(w[0], w[4]))
+            return top
+        return jnp.max(lax.fori_loop(0, 8, body, jnp.zeros((8, fluid.shape[-1]), F32)))
+
+    def states(before, here, after):
+        low, high = [], []
+        for a, b, c in zip(before, here, after):
+            p, q = b - a, c - b
+            half_slope = 0.5 * (
+                jnp.maximum(0.0, jnp.minimum(p, q)) + jnp.minimum(0.0, jnp.maximum(p, q))
+            )
+            low.append(b - half_slope)
+            high.append(b + half_slope)
+        return low, high
+
+    def side(w, n):
+        dens, vel, pres = w[0], w[1:4], w[4]
+        energy = pres * (1.0 / (GAMMA - 1.0)) + 0.5 * dens * (
+            vel[0] * vel[0] + vel[1] * vel[1] + vel[2] * vel[2]
+        )
+        mom = [dens * v for v in vel]
+        flux = [mom[n]] + [mom[n] * v for v in vel] + [(energy + pres) * vel[n]]
+        flux[1 + n] = flux[1 + n] + pres
+        return [dens] + mom + [energy], flux, jnp.abs(vel[n]) + sound(dens, pres)
+
+    def face(left, right, n):
+        cl, fl, al = side(left, n)
+        cr, fr, ar = side(right, n)
+        top = jnp.maximum(al, ar)
+        return [0.5 * ((a + b) - top * (d - c)) for a, b, c, d in zip(fl, fr, cl, cr)]
+
+    def sweep_line(get, put, n):
+        w = [get(0), get(1), get(2)]
+        _, high = states(*w)
+        flux = None
+        for i in range(2, 11):
+            w = [w[1], w[2], get(i + 1)]
+            low, high_next = states(*w)
+            now = face(high, low, n)
+            if flux is not None:
+                put(i - 3, [b - a for a, b in zip(flux, now)])
+            flux, high = now, high_next
+
+    def lines_x(y, _):
+        def get(i):
+            return [prim[v, i, y + 2] for v in range(5)]
+
+        def put(i, values):
+            for v in range(5):
+                change[v, i, y] = values[v]
+
+        sweep_line(get, put, 0)
+        return 0
+
+    def lines_y(x, _):
+        def get(i):
+            return [prim[v, x + 2, i] for v in range(5)]
+
+        def put(i, values):
+            for v in range(5):
+                change[v, x, i] += values[v]
+
+        sweep_line(get, put, 1)
+        return 0
+
+    def last_faces(x, _):
+        w = [
+            cell_values([fluid[v, x + 2, cells, k, :] for v in range(5)]) for k in (8, 9, 10, 11)
+        ]
+        _, high = states(w[0], w[1], w[2])
+        low, _ = states(w[1], w[2], w[3])
+        flux = face(high, low, 2)
+        for v in range(5):
+            last_face[v, x] = flux[v]
+        return 0
+
+    def lines_z(x, _):
+        row = lax.broadcasted_iota(jnp.int32, (8, fluid.shape[-1]), 0)
+        for y in range(8):
+            w = [
+                cell_values([fluid[v, x + 2, y + 2, pl.ds(k, 8), :] for v in range(5)]) if k != 2
+                else [prim[v, x + 2, y + 2] for v in range(5)]
+                for k in range(4)
+            ]
+            _, high = states(w[0], w[1], w[2])
+            low, _ = states(w[1], w[2], w[3])
+            flux = face(high, low, 2)
+            for v in range(5):
+                after = jnp.where(row == 7, last_face[v, x, pl.ds(y, 1), :], pltpu.roll(flux[v], 7, 0))
+                change[v, x, y] += after - flux[v]
+        return 0
+
     pl.semaphore_wait(barrier, ng + nf - 2)
 
-    def send(axis, pos, count, source, target, sends, recvs):
+    def grp_partner(i, way):
+        return lax.rem(g + way * i + ng, ng), i
+
+    def fft_partner(i, way):
+        a, b = i // ny_chips, lax.rem(i, ny_chips)
+        dz = nz_chips // 2 + ((a + 1) // 2) * (1 - 2 * lax.rem(a, 2))
+        dy = ny_chips // 2 + ((b + 1) // 2) * (1 - 2 * lax.rem(b, 2))
+        z = lax.rem(f // ny_chips + way * dz + nz_chips, nz_chips)
+        y = lax.rem(lax.rem(f, ny_chips) + way * dy + ny_chips, ny_chips)
+        return z * ny_chips + y, i
+
+    ways = {"grp": (1, ng, grp_partner, g), "fft": (0, nf - 1, fft_partner, f)}
+
+    def send(axis, source, target, sends, recvs):
+        begin, end, partner, pos = ways[axis]
+
         def body(k, _):
-            to = lax.rem(pos + k, count)
+            to, at = partner(k, 1)
             pltpu.make_async_remote_copy(
-                source(to), target(pos), sends.at[k], recvs.at[k], device_id={axis: to},
+                source(to), target(pos), sends.at[at], recvs.at[at], device_id={axis: to},
                 device_id_type=pl.DeviceIdType.MESH,
             ).start()
             return 0
-        lax.fori_loop(1, count, body, 0)
-
-    def receive(axis, pos, count, source, target, sends, recvs):
+
+        lax.fori_loop(begin, end, body, 0)
+
+    def receive(axis, source, target, sends, recvs):
+        begin, end, partner, pos = ways[axis]
+
         def body(k, _):
-            come = lax.rem(pos + (count - k), count)
+            come, at = partner(k, -1)
             pltpu.make_async_remote_copy(
-                source(come), target(come), sends.at[k], recvs.at[k], device_id={axis: come},
+                source(come), target(come), sends.at[at], recvs.at[at], device_id={axis: come},
                 device_id_type=pl.DeviceIdType.MESH,
-            ).wait()
+            ).wait_recv()
             return 0
-        lax.fori_loop(1, count, body, 0)
+
+        lax.fori_loop(begin, end, body, 0)
+
+    def sent(axis, source, target, sends, recvs):
+        begin, end, partner, pos = ways[axis]
+
+        def body(k, _):
+            to, at = partner(k, 1)
+            pltpu.make_async_remote_copy(
+                source(to), target(pos), sends.at[at], recvs.at[at], device_id={axis: to},
+                device_id_type=pl.DeviceIdType.MESH,
+            ).wait_send()
+            return 0
+
+        lax.fori_loop(begin, end, body, 0)
 
     slice1 = lambda d: s1.at[:, pl.ds(pl.multiple_of(d * kz, kz), kz), :]
-    ex1 = ("grp", g, ng, slice1, lambda d: r1.at[d], s1s, r1s)
+    ex1 = ("grp", slice1, lambda d: r1.at[d], s1s, r1s)
     send(*ex1)
     r1[g] = s1[:, pl.ds(pl.multiple_of(g * kz, kz), kz), :]
 
@@ -278,6 +429,9 @@
         return m1
 
     lax.fori_loop(0, nf, coefficients, jnp.zeros((8, 128), F32))
+    loads["fluid"].wait()
+    lax.fori_loop(0, 12, make_cells, 0)
+    most = jnp.full((1, 128), top_speed(), F32)
     loads["wide"].wait()
     loads["sx"].wait()
     loads["edge"].wait()
@@ -288,8 +442,6 @@
     main = dot_right(main, wide[0], wide[1])
     across = r1[...].reshape(ng * 2 * kz, 128).T
     edge_x = across[cy : cy + cx]
-    most = across[cy + cx : cy + cx + 8]
-    most = jnp.max(jnp.maximum(most[:, :128], most[:, 128:]), axis=0, keepdims=True)
     edge_k = jnp.dot(sx[...], edge_x, precision=lax.Precision.HIGHEST, preferred_element_type=F32)
     wide_lane = ng * 2 * kz
     diag = (
@@ -318,13 +470,14 @@
         s2[pl.ds(r, nf, stride=8), :] = jnp.broadcast_to(most, (nf, 128))
 
     tile = lambda ref: lambda d: ref.at[pl.ds(pl.multiple_of(d * 8, 8), 8), :]
-    ex2 = ("fft", f, nf, tile(s2), tile(r2), s2s, r2s)
+    ex2 = ("fft", tile(s2), tile(r2), s2s, r2s)
     send(*ex2)
     mine = pl.ds(pl.multiple_of(f * 8, 8), 8)
     r2[mine, :] = s2[mine, :]
+    lax.fori_loop(0, 8, lines_x, 0)
+    lax.fori_loop(0, 8, lines_y, 0)
     receive(*ex2)
-    most = jnp.max(r2[pl.ds(6, nf, stride=8), :])
-    step = COURANT * FINE_STEP / most
+    most = jnp.max(r2[pl.ds(6, nf, stride=8), :], axis=0, keepdims=True)
 
     last = jnp.zeros((8, 128), F32)
     prev = last
@@ -345,11 +498,13 @@
         right = chain[2 * d + 2] if d < nf - 1 else last
         s3[8 * d : 8 * d + 8, :] = jnp.where(sub < 3, left, pltpu.roll(right, 3, 0))
 
-    ex3 = ("fft", f, nf, tile(s3), tile(r3), s3s, r3s)
+    ex3 = ("fft", tile(s3), tile(r3), s3s, r3s)
     send(*ex3)
     r3[mine, :] = s3[mine, :]
     loads["edget"].wait()
     loads["back"].wait()
+    lax.fori_loop(0, 8, last_faces, 0)
+    lax.fori_loop(0, 8, lines_z, 0)
     receive(*ex3)
     around = [
         jnp.concatenate(
@@ -377,15 +532,22 @@
     sides = jnp.concatenate(
         [jnp.zeros((cy, wide_lane), F32), sides, jnp.zeros((128 - cy - cx, wide_lane), F32)], axis=0
     ).T
+    sides = jnp.where(
+        lax.broadcasted_iota(jnp.int32, (wide_lane, 128), 1) == 127, jnp.broadcast_to(most, (wide_lane, 128)), sides
+    )
     for d in range(ng):
         s4[d] = (out_rows[:, 128 * d : 128 * d + 128] + sides[2 * kz * d : 2 * kz * (d + 1)]).reshape(2, kz, 128)
 
-    ex4 = ("grp", g, ng, lambda d: s4.at[d], lambda d: r4.at[:, d], s4s, r4s)
+    ex4 = ("grp", lambda d: s4.at[d], lambda d: r4.at[:, d], s4s, r4s)
     send(*ex4)
     r4[:, g] = s4[g]
+    sent(*ex1)
+    sent(*ex2)
+    sent(*ex3)
     receive(*ex4)
     for e in range(2):
         solved[e] = r4[e].reshape(nz, 128).T
+    most_out[...] = jnp.full((8, 128), jnp.max(solved[0, pl.ds(127, 1), :]), F32)
 
     def second_solve(i, _):
         def fetch(x, at):
@@ -440,7 +602,6 @@
             grid[(cx + 1) * e, pl.ds(7 if s == 0 else 8 + cy, 1), :] = lines[cx + s : cx + s + 1]
 
     loads["fold"].wait()
-    loads["weave"].wait()
     per_y, per_z = cy // 4, nz // 4
     lanes8 = lax.broadcasted_iota(jnp.int32, (8, 128), 1)
     pick = (
@@ -478,28 +639,69 @@
 
     lax.fori_loop(0, nf // some, gather, 0)
 
-    ex6 = ("fft", f, nf, tile(s6), tile(r6), s6s, r6s)
+    ex6 = ("fft", tile(s6), tile(r6), s6s, r6s)
     send(*ex6)
     r6[mine, :] = s6[mine, :]
+    sent(*ex4)
+    copy_out.wait()
     receive(*ex6)
-    lanes = lax.broadcasted_iota(jnp.int32, (nf, 128), 1)
+    blocks[...] = r6[...]
+    sent(*ex6)
+
+
+def patch_kernel(
+    blocks, most, change_h, fluid_h, pot_in, weave,
+    fine, moved, pot_out,
+    fluid, change, force, state, hold, sems,
+):
+    count = fine.shape[-1]
+    nf = blocks.shape[0] // 8
+    copies = [
+        pltpu.make_async_copy(fluid_h.at[0], fluid.at[0], sems.at[0]),
+        pltpu.make_async_copy(pot_in, hold, sems.at[1]),
+        pltpu.make_async_copy(change_h, change, sems.at[2]),
+        pltpu.make_async_copy(fluid_h.at[pl.ds(1, 4)], fluid.at[pl.ds(1, 4)], sems.at[3]),
+    ]
+    for c in copies:
+        c.start()
+    copy_out = pltpu.make_async_copy(hold, pot_out, sems.at[4])
+    groups = 128 // count
+
+    lanes = lax.rem(lax.broadcasted_iota(jnp.int32, (nf, 128), 1), count)
     hot = jnp.concatenate(
         [
-            jnp.where(r6[pl.ds(6 + c, nf, stride=8), :] == lanes.astype(F32), 1.0, 0.0)
+            jnp.where(blocks[pl.ds(6 + c, nf, stride=8), :] == lanes.astype(F32), 1.0, 0.0)
             for c in range(2)
         ],
         axis=0,
     ).astype(BF16)
     within, outside = [], []
     for t in range(3):
-        came = jnp.concatenate([r6[pl.ds(c * 3 + t, nf, stride=8), :] for c in range(2)], axis=0)
+        came = jnp.concatenate([blocks[pl.ds(c * 3 + t, nf, stride=8), :] for c in range(2)], axis=0)
         a, b = split(came.T)
         placed = mm(a, hot) + mm(b, hot)
         a, b = split(placed)
         woven = mm(weave[...], a) + mm(weave[...], b)
-        woven = woven.reshape(2, 2, 8, 8, 128)[..., : fine.shape[-1]]
+        woven = woven.reshape(2, 2, 8, 8, 128)
         within += [woven[0, 0], woven[0, 1]]
         outside += [woven[1, 0], woven[1, 1]]
+
+    z = lax.broadcasted_iota(jnp.int32, (8, 128), 0)
+    q = lax.broadcasted_iota(jnp.int32, (8, 128), 1) // count
+    bottom, top, zeven = z == 0, z == 7, lax.rem(z, 2) == 0
+    zodd = jnp.logical_not(zeven)
+    first, final = q == 0, q == 3
+
+    def choose(values, shift, y):
+        out = values[shift + 3][y]
+        for i in (2, 1, 0):
+            out = jnp.where(q == i, values[shift + i][y], out)
+        return out
+
+    def along_x(values, r, y):
+        if r == 0:
+            return 0.25 * choose(values, 0, y) + 0.75 * choose(values, 1, y)
+        return 0.75 * choose(values, 1, y) + 0.25 * choose(values, 2, y)
 
     def between(values, j):
         low = j // 2
@@ -509,75 +711,102 @@
             else 0.25 * values[low] + 0.75 * values[low + 1]
         )
 
+    copies[0].wait()
     scale = 1.0 / (6.0 + SCREEN * FINE_STEP * FINE_STEP)
-    for jx in range(10):
-        plane = between(within, jx)
+    layers = {}
+    rims = {}
+    for r in range(2):
+        plane = [along_x(within, r, y) for y in range(6)]
         for jy in range(10):
-            field[jx, jy] = between(plane, jy)
-        if 1 <= jx <= 8:
-            plane = between(outside, jx)
-            for jy in range(1, 9):
-                layer = between(plane, jy)
-                ghosts[jx - 1, jy - 1] = layer
-                force[jx - 1, jy - 1] = (OMEGA * scale) * (
-                    layer - FINE_STEP * FINE_STEP * fluid[0, jx - 1, jy - 1]
-                )
-
-    width = fine.shape[-1]
-    z = lax.broadcasted_iota(jnp.int32, (8, width), 0)
-    bottom, top, zeven = z == 0, z == 7, lax.rem(z, 2) == 0
-    zodd = jnp.logical_not(zeven)
+            value = between(plane, jy)
+            if 1 <= jy <= 8:
+                state[r, jy - 1] = value
+            else:
+                rims[r, jy] = value
+        plane = [along_x(outside, r, y) for y in range(6)]
+        for jy in range(1, 9):
+            layers[r, jy - 1] = between(plane, jy)
+    ends = (
+        [0.75 * within[0][y] + 0.25 * within[1][y] for y in range(6)],
+        [0.25 * within[4][y] + 0.75 * within[5][y] for y in range(6)],
+    )
+    for r in range(2):
+        for y in range(8):
+            rho = jnp.concatenate(
+                [fluid[0, 2 * i + r + 2, y + 2, pl.ds(2, 8), :] for i in range(groups)], axis=1
+            )
+            side = jnp.where(first if r == 0 else final, between(ends[r], y + 1), 0.0)
+            ghost = layers[r, y] + side
+            if y == 0:
+                ghost = ghost + rims[r, 0]
+            if y == 7:
+                ghost = ghost + rims[r, 9]
+            force[r, y] = (OMEGA * scale) * (ghost - FINE_STEP * FINE_STEP * rho)
+
+    copies[1].wait()
+    copy_out.start()
+
+    def beside(r, y, v):
+        other = state[1 - r, y]
+        if r == 0:
+            far = jnp.where(first, 0.0, pltpu.roll(other, count, 1))
+        else:
+            far = jnp.where(final, 0.0, pltpu.roll(other, 128 - count, 1))
+        return other, far
 
     def sweep(_, carry):
         for colour in (0, 1):
-            def planes(i, c, colour=colour):
-                for k in range(2):
-                    x = 2 * i + k + 1
-                    for y in range(1, 9):
-                        v = field[x, y]
-                        near = (
-                            (field[x - 1, y] + field[x + 1, y])
-                            + (field[x, y - 1] + field[x, y + 1])
-                            + (
-                                jnp.where(bottom, 0.0, pltpu.roll(v, 1, 0))
-                                + jnp.where(top, 0.0, pltpu.roll(v, 7, 0))
-                            )
-                        )
-                        new = (1.0 - OMEGA) * v + ((OMEGA * scale) * near + force[x - 1, y - 1])
-                        mask = zeven if (k + y - 1 + colour) % 2 == 0 else zodd
-                        field[x, y] = jnp.where(mask, new, v)
-                return c
-            lax.fori_loop(0, 4, planes, 0)
+            for r in range(2):
+                for y in range(8):
+                    v = state[r, y]
+                    other, far = beside(r, y, v)
+                    near = (other + far) + (
+                        jnp.where(bottom, 0.0, pltpu.roll(v, 1, 0)) + jnp.where(top, 0.0, pltpu.roll(v, 7, 0))
+                    )
+                    if y > 0:
+                        near = near + state[r, y - 1]
+                    if y < 7:
+                        near = near + state[r, y + 1]
+                    new = (1.0 - OMEGA) * v + ((OMEGA * scale) * near + force[r, y])
+                    mask = zeven if (r + y + colour) % 2 == 0 else zodd
+                    state[r, y] = jnp.where(mask, new, v)
         return carry
 
     lax.fori_loop(0, SWEEPS, sweep, 0)
 
-    def update(x, _):
+    copies[2].wait()
+    copies[3].wait()
+    step = COURANT * FINE_STEP / most[pl.ds(0, 1), pl.ds(0, count)]
+    rate = step / FINE_STEP
+    for r in range(2):
         for y in range(8):
-            v = field[x + 1, y + 1]
-            layer = ghosts[x, y]
-            fine[x, y] = v
+            v = state[r, y]
+            other, far = beside(r, y, v)
+            far = far + jnp.where(first if r == 0 else final, between(ends[r], y + 1), 0.0)
+            layer = layers[r, y]
+            down = state[r, y - 1] if y > 0 else rims[r, 0]
+            up = state[r, y + 1] if y < 7 else rims[r, 9]
             pull = (
-                field[x, y + 1] - field[x + 2, y + 1],
-                field[x + 1, y] - field[x + 1, y + 2],
+                far - other if r == 0 else other - far,
+                down - up,
                 jnp.where(bottom, layer, pltpu.roll(v, 1, 0)) - jnp.where(top, layer, pltpu.roll(v, 7, 0)),
             )
-            dens = fluid[0, x, y]
-            rate = step / FINE_STEP
-            work = 0.0
-            moved[0, x, y] = dens - rate * change[0, x, y]
-            for n in range(3):
-                mom = fluid[1 + n, x, y]
-                moved[1 + n, x, y] = mom - rate * change[1 + n, x, y] + step * dens * pull[n]
-                work = work + mom * pull[n]
-            moved[4, x, y] = fluid[4, x, y] - rate * change[4, x, y] + step * work
-        return 0
-
-    lax.fori_loop(0, 8, update, 0)
+            for i in range(groups):
+                x = 2 * i + r
+                at = slice(count * i, count * (i + 1))
+                fine[x, y] = v[:, at]
+                cons = [fluid[k, x + 2, y + 2, pl.ds(2, 8), :] for k in range(5)]
+                work = 0.0
+                moved[0, x, y] = cons[0] - rate * change[0, x, y]
+                for n in range(3):
+                    force_n = pull[n][:, at]
+                    moved[1 + n, x, y] = cons[1 + n] - rate * change[1 + n, x, y] + step * cons[0] * force_n
+                    work = work + cons[1 + n] * force_n
+                moved[4, x, y] = cons[4] - rate * change[4, x, y] + step * work
     copy_out.wait()
 
 
-def root_call(ghost, rho, speed, fluid, change, nf, ng):
+def root_call(ghost, rho, fluid, nf, ng):
     cx, cy, nz = rho.shape
     kz = nz // ng
     ny = ng * cy
@@ -591,19 +820,21 @@
     local = {n: tab[n].shape for n in NAMES}
     local["inv"] = local["inv"][1:]
     local["pair"] = local["pair"][2:]
-    return pl.pallas_call(
+    limit = 56 * 1024 * 1024
+    potential, blocks, most, change = pl.pallas_call(
         functools.partial(root_kernel, (nf, ng, cx, cy, nz)),
         out_shape=(
             jax.ShapeDtypeStruct((cx, cy, nz), F32),
-            jax.ShapeDtypeStruct((8, 8, 8, count), F32),
+            jax.ShapeDtypeStruct((nf * 8, 128), F32),
+            jax.ShapeDtypeStruct((8, 128), F32),
             jax.ShapeDtypeStruct((5, 8, 8, 8, count), F32),
         ),
-        in_specs=[pl.BlockSpec(memory_space=pltpu.SMEM), anyspace, vspace, vspace, vspace]
-        + [anyspace] * len(NAMES),
-        out_specs=(anyspace, vspace, vspace),
+        in_specs=[pl.BlockSpec(memory_space=pltpu.SMEM)] + [anyspace] * (2 + len(NAMES)),
+        out_specs=(anyspace, vspace, vspace, vspace),
         scratch_shapes=[vm((cx, cy, nz))]
         + [vm(local[n], consts[i].dtype) for i, n in enumerate(NAMES)]
         + [
+            vm(fluid.shape), vm((5, 12, 12, 8, count)),
             vm((cx, cy, nz)),
             vm((2, 128, nz)),
             vm((cx, 8, nz)),
@@ -615,7 +846,7 @@
             vm((ng, 2, kz, 128)), vm((2, ng, kz, 128)),
             vm((nf * 8, 128)), vm((nf * 8, 128)),
             vm((2 * nf, 8, 128)), vm((2 * nf, 8, 128)),
-            vm((10, 10, 8, count)), vm((8, 8, 8, count)), vm((8, 8, 8, count)),
+            vm((5, 8, 8, count)),
             dma((14,)), dma,
             dma((ng,)), dma((ng,)),
             dma((nf,)), dma((nf,)),
@@ -624,73 +855,32 @@
             dma((nf,)), dma((nf,)),
         ],
         compiler_params=pltpu.CompilerParams(
-            collective_id=0, has_side_effects=True, vmem_limit_bytes=56 * 1024 * 1024
+            collective_id=0, has_side_effects=True, vmem_limit_bytes=limit
         ),
-    )(ghost, rho, speed, fluid, change, *consts)
-
-
-def primitives(fluid):
-    dens = fluid[0]
-    vel = fluid[1:4] / dens
-    kinetic = 0.5 * jnp.sum(fluid[1:4] * vel, axis=0)
-    pres = (GAMMA - 1.0) * (fluid[4] - kinetic)
-    return (dens, vel, pres)
-
-
-def signal_speed(fluid):
-    dens, vel, pres = primitives(fluid[:, 2:10, 2:10, 2:10])
-    sound = jnp.sqrt(GAMMA * pres / dens)
-    return jnp.max(jnp.max(jnp.abs(vel), axis=0) + sound)
-
-
-def along(array, axis, start, stop):
-    return lax.slice_in_dim(array, start, stop, axis=axis + 1)
-
-
-def conserved_flux(state, axis):
-    dens = state[0]
-    vel = state[1:4]
-    pres = state[4]
-    normal = vel[axis]
-    energy = pres / (GAMMA - 1.0) + 0.5 * dens * jnp.sum(vel * vel, axis=0)
-    cons = jnp.stack([dens, dens * vel[0], dens * vel[1], dens * vel[2], energy])
-    moment = [dens * normal * vel[other] + (pres if other == axis else 0.0) for other in range(3)]
-    flux = jnp.stack([dens * normal, moment[0], moment[1], moment[2], (energy + pres) * normal])
-    speed = jnp.abs(normal) + jnp.sqrt(GAMMA * pres / dens)
-    return (cons, flux, speed)
-
-
-def flux_difference(prim, axis):
-    for other in range(3):
-        if other != axis:
-            prim = along(prim, other, 2, 10)
-    left_diff = along(prim, axis, 1, 11) - along(prim, axis, 0, 10)
-    right_diff = along(prim, axis, 2, 12) - along(prim, axis, 1, 11)
-    slope = (
-        0.5
-        * (jnp.sign(left_diff) + jnp.sign(right_diff))
-        * jnp.minimum(jnp.abs(left_diff), jnp.abs(right_diff))
-    )
-    centre = along(prim, axis, 1, 11)
-    upper = centre + 0.5 * slope
-    lower = centre - 0.5 * slope
-    cons_left, flux_left, speed_left = conserved_flux(along(upper, axis, 0, 9), axis)
-    cons_right, flux_right, speed_right = conserved_flux(along(lower, axis, 1, 10), axis)
-    flux = 0.5 * (flux_left + flux_right) - 0.5 * jnp.maximum(speed_left, speed_right) * (
-        cons_right - cons_left
-    )
-    return along(flux, axis, 1, 9) - along(flux, axis, 0, 8)
+    )(ghost, rho, fluid, *consts)
+    fine, moved, potential = pl.pallas_call(
+        patch_kernel,
+        out_shape=(
+            jax.ShapeDtypeStruct((8, 8, 8, count), F32),
+            jax.ShapeDtypeStruct((5, 8, 8, 8, count), F32),
+            jax.ShapeDtypeStruct((cx, cy, nz), F32),
+        ),
+        in_specs=[vspace, vspace, anyspace, anyspace, anyspace, vspace],
+        out_specs=(vspace, vspace, anyspace),
+        scratch_shapes=[
+            vm(fluid.shape), vm((5, 8, 8, 8, count)),
+            vm((2, 8, 8, 128)), vm((2, 8, 8, 128)), vm((cx, cy, nz)),
+            dma((5,)),
+        ],
+        compiler_params=pltpu.CompilerParams(vmem_limit_bytes=limit),
+    )(blocks, most, change, fluid, potential, jnp.asarray(tab["weave"]))
+    return potential, fine, moved
 
 
 def per_device(root_density, patch_fluid, ghost_list):
     nf = lax.axis_size("fft")
     ng = lax.axis_size("grp")
-    speed = jnp.broadcast_to(signal_speed(patch_fluid), (8, 128))
-    dens, vel, pres = primitives(patch_fluid)
-    prim = jnp.concatenate([dens[None], vel, pres[None]], axis=0)
-    change = flux_difference(prim, 0) + flux_difference(prim, 1) + flux_difference(prim, 2)
-    inner = patch_fluid[:, 2:10, 2:10, 2:10]
-    return root_call(ghost_list[:, 0], root_density, speed, inner, change, nf, ng)
+    return root_call(ghost_list[:, 0], root_density, patch_fluid, nf, ng)
 
 
 def solution(mesh):

time: 97.7 us -> 65.6 us (0.67)
  other arithmetic: 19.3 us -> 0 us
  local copies, waits for them, and re-layouts: 8.51 us -> 0 us
  Pallas kernels: 68.7 us -> 64.9 us
    pallas_call x1, Pallas kernels: 68.7 us -> 57.9 us  [root_call(): pl.pallas_call(functools.partial(root_kernel, (nf, ng, cx, cy, nz)), out_...]
    pallas_call x0 -> x1, Pallas kernels: none -> 7.02 us  [root_call(): pl.pallas_call(patch_kernel, out_shape=(jax.ShapeDtypeStruct((8, 8, 8, co...]
    add x4 -> x0, other arithmetic: 6.56 us -> none  [the longest x3 5.12 us: flux_difference(): upper = centre + 0.5 * slope]
    unnamed x17 -> x0, local copies, waits for them, and re-layouts: 4.43 us -> none
    reduce_sum x5 -> x0, other arithmetic: 4.38 us -> none  [the longest x2 3.26 us: primitives(): kinetic = 0.5 * jnp.sum(fluid[1:4] * vel, axis=0)]
    slice x2 -> x0, local copies, waits for them, and re-layouts: 2.81 us -> none  [the longest x1 1.57 us: primitives(): dens = fluid[0]]
    unnamed x28 -> x0, other arithmetic: 2.33 us -> none
    sub x3 -> x0, other arithmetic: 2.3 us -> none  [flux_difference(): 0.5 * (flux_left + flux_right)]
where the time goes in v2:
time: 65.6 us; the launch traced here: 65.5 us
  Pallas kernels  64.9 us (99%)
    pallas_call x1, Pallas kernels, root_call(): pl.pallas_call(functools.partial(root_kernel, (nf, ng, cx, cy, nz)), out_...  57.9 us
    pallas_call x1, Pallas kernels, root_call(): pl.pallas_call(patch_kernel, out_shape=(jax.ShapeDtypeStruct((8, 8, 8, co...  7.02 us

profile of v2, /device:TPU:1, one launch (start us, length us, event | category | flops | bytes accessed | tf_op | source)
XLA Modules:
  0.0 65.5 jit_solution(6073804755244788434)
XLA Ops:
  0.6 57.9 %shard_map.175 = (f32[24,96,128]{2,1,0:T(8,128)}, f32[256,128]{1,0:T(8,128)}, f32[8,128]{1,0:T(8,128)}, f32[5,8,8,8,32]{4,3,2,1,0:T(8,128)}) custom-call(s32[2,64]{1,0:T(2,128)} %bitcast.1, f32[24,96,128]{2,1,0:T(8,128)} %rho.1, f32[5,12,12,12,32]{4,3,2,1,0:T(8,128)} %fluid_h.3, bf16[256,256]{1,0:T(8,128)(2,1)} %constant.26.clone.sz_h, ...), custom_call_target="tpu_custom_call" | custom-call | tf_op jit(solution)/shard_map/pallas_call | solution.py:824
  58.5 7.0 %shard_map.176 = (f32[8,8,8,32]{3,2,1,0:T(8,128)}, f32[5,8,8,8,32]{4,3,2,1,0:T(8,128)}, f32[24,96,128]{2,1,0:T(8,128)}) custom-call(f32[256,128]{1,0:T(8,128)} %get-tuple-element.10.blocks, f32[8,128]{1,0:T(8,128)} %get-tuple-element.11.most, f32[5,8,8,8,32]{4,3,2,1,0:T(8,128)} %get-tuple-element.12.change_h, f32[5,12,12,12,32]{4,3,2,1,0:T(8,128)} %fluid_h.3, ...), custom_call_target="tpu_custom_call" | custom-call | tf_op jit(solution)/shard_map/pallas_call | solution.py:861

commit v3 on v2

--- a/solution.py
+++ b/solution.py
@@ -92,7 +92,7 @@
     szh, szl = halves(sz)
     return dict(
         sz=np.block([[szh, szl], [szh, np.zeros_like(szh)]]).astype(ml_dtypes.bfloat16),
-        sy=halves(sy),
+        sy=np.concatenate(halves(sy)),
         sx=as32(sx),
         steps=as32(np.stack(steps)),
         wide=halves(wide.reshape(ng * 128, ny)),
@@ -126,9 +126,11 @@
     return mm(a, high) + (mm(b, high) + mm(a, low))
 
 
-def dot_left(high, low, value):
+def dot_left(both, value):
+    rows = both.shape[0] // 2
     a, b = split(value)
-    return mm(high, a) + (mm(high, b) + mm(low, a))
+    main = mm(both, a)
+    return main[:rows] + (main[rows:] + mm(both[:rows], b))
 
 
 def root_kernel(
@@ -139,7 +141,7 @@
     src, sz, sy, sx, steps, wide, back, edge, edget, inv, pair, fold, column, fluid, prim,
     block, solved, part, grid, hfield,
     s1, r1, s2, r2, s3, r3, s4, r4, s6, r6, chain, mults, last_face,
-    tsem, osem, s1s, r1s, s2s, r2s, s3s, r3s, s4s, r4s, s6s, r6s,
+    tsem, osem, x1, x2, x3, x4, x6,
 ):
     nf, ng, cx, cy, nz = cfg
     kz = nz // ng
@@ -152,17 +154,30 @@
     nz_chips = nf // ny_chips
     barrier = pltpu.get_barrier_semaphore()
 
-    def hello(axis, pos, count):
+    def grp_partner(k):
+        return lax.rem(g + k, ng)
+
+    def fft_partner(k):
+        a, b = k // ny_chips, lax.rem(k, ny_chips)
+        dz = nz_chips // 2 + ((a + 1) // 2) * (1 - 2 * lax.rem(a, 2))
+        dy = ny_chips // 2 + ((b + 1) // 2) * (1 - 2 * lax.rem(b, 2))
+        return lax.rem(f // ny_chips + dz, nz_chips) * ny_chips + lax.rem(lax.rem(f, ny_chips) + dy, ny_chips)
+
+    ways = {"grp": (1, ng, grp_partner, g), "fft": (0, nf - 1, fft_partner, f)}
+
+    def hello(axis):
+        begin, end, partner, _ = ways[axis]
+
         def body(k, _):
             pl.semaphore_signal(
-                barrier, inc=1, device_id={axis: lax.rem(pos + k, count)},
-                device_id_type=pl.DeviceIdType.MESH,
+                barrier, inc=1, device_id={axis: partner(k)}, device_id_type=pl.DeviceIdType.MESH
             )
             return 0
-        lax.fori_loop(1, count, body, 0)
-
-    hello("grp", g, ng)
-    hello("fft", f, nf)
+
+        lax.fori_loop(begin, end, body, 0, unroll=True)
+
+    hello("fft")
+    hello("grp")
 
     loads = {}
     order = [
@@ -188,12 +203,12 @@
         both = mm(jnp.concatenate([a, b], axis=1), sz[...])
         both = both[:, :nz] + both[:, nz:]
         pair_x = jnp.concatenate([both[:cy], both[cy:]], axis=1)
-        out = dot_left(sy[0], sy[1], pair_x)
+        out = dot_left(sy[...], pair_x)
         block[2 * i] = out[:, :nz]
         block[2 * i + 1] = out[:, nz:]
         return 0
 
-    lax.fori_loop(0, half, forward, 0)
+    lax.fori_loop(0, half, forward, 0, unroll=3)
 
     loads["steps"].wait()
     loads["column"].wait()
@@ -360,60 +375,33 @@
 
     pl.semaphore_wait(barrier, ng + nf - 2)
 
-    def grp_partner(i, way):
-        return lax.rem(g + way * i + ng, ng), i
-
-    def fft_partner(i, way):
-        a, b = i // ny_chips, lax.rem(i, ny_chips)
-        dz = nz_chips // 2 + ((a + 1) // 2) * (1 - 2 * lax.rem(a, 2))
-        dy = ny_chips // 2 + ((b + 1) // 2) * (1 - 2 * lax.rem(b, 2))
-        z = lax.rem(f // ny_chips + way * dz + nz_chips, nz_chips)
-        y = lax.rem(lax.rem(f, ny_chips) + way * dy + ny_chips, ny_chips)
-        return z * ny_chips + y, i
-
-    ways = {"grp": (1, ng, grp_partner, g), "fft": (0, nf - 1, fft_partner, f)}
-
-    def send(axis, source, target, sends, recvs):
+    def send(axis, source, target, every, sems):
         begin, end, partner, pos = ways[axis]
 
         def body(k, _):
-            to, at = partner(k, 1)
+            to = partner(k)
             pltpu.make_async_remote_copy(
-                source(to), target(pos), sends.at[at], recvs.at[at], device_id={axis: to},
+                source(to), target(pos), sems.at[0], sems.at[1], device_id={axis: to},
                 device_id_type=pl.DeviceIdType.MESH,
             ).start()
             return 0
 
-        lax.fori_loop(begin, end, body, 0)
-
-    def receive(axis, source, target, sends, recvs):
-        begin, end, partner, pos = ways[axis]
-
-        def body(k, _):
-            come, at = partner(k, -1)
-            pltpu.make_async_remote_copy(
-                source(come), target(come), sends.at[at], recvs.at[at], device_id={axis: come},
-                device_id_type=pl.DeviceIdType.MESH,
-            ).wait_recv()
-            return 0
-
-        lax.fori_loop(begin, end, body, 0)
-
-    def sent(axis, source, target, sends, recvs):
-        begin, end, partner, pos = ways[axis]
-
-        def body(k, _):
-            to, at = partner(k, 1)
-            pltpu.make_async_remote_copy(
-                source(to), target(pos), sends.at[at], recvs.at[at], device_id={axis: to},
-                device_id_type=pl.DeviceIdType.MESH,
-            ).wait_send()
-            return 0
-
-        lax.fori_loop(begin, end, body, 0)
+        lax.fori_loop(begin, end, body, 0, unroll=True)
+
+    def whole(axis, source, target, every, sems):
+        return pltpu.make_async_remote_copy(
+            every, every, sems.at[0], sems.at[1], device_id={axis: ways[axis][2](1)},
+            device_id_type=pl.DeviceIdType.MESH,
+        )
+
+    def receive(*exchange):
+        whole(*exchange).wait_recv()
+
+    def sent(*exchange):
+        whole(*exchange).wait_send()
 
     slice1 = lambda d: s1.at[:, pl.ds(pl.multiple_of(d * kz, kz), kz), :]
-    ex1 = ("grp", slice1, lambda d: r1.at[d], s1s, r1s)
+    ex1 = ("grp", slice1, lambda d: r1.at[d], r1.at[pl.ds(0, ng - 1)], x1)
     send(*ex1)
     r1[g] = s1[:, pl.ds(pl.multiple_of(g * kz, kz), kz), :]
 
@@ -469,8 +457,9 @@
     for r in (6, 7):
         s2[pl.ds(r, nf, stride=8), :] = jnp.broadcast_to(most, (nf, 128))
 
+    most_rows = lambda ref: ref.at[pl.ds(0, (nf - 1) * 8), :]
     tile = lambda ref: lambda d: ref.at[pl.ds(pl.multiple_of(d * 8, 8), 8), :]
-    ex2 = ("fft", tile(s2), tile(r2), s2s, r2s)
+    ex2 = ("fft", tile(s2), tile(r2), most_rows(r2), x2)
     send(*ex2)
     mine = pl.ds(pl.multiple_of(f * 8, 8), 8)
     r2[mine, :] = s2[mine, :]
@@ -498,7 +487,7 @@
         right = chain[2 * d + 2] if d < nf - 1 else last
         s3[8 * d : 8 * d + 8, :] = jnp.where(sub < 3, left, pltpu.roll(right, 3, 0))
 
-    ex3 = ("fft", tile(s3), tile(r3), s3s, r3s)
+    ex3 = ("fft", tile(s3), tile(r3), most_rows(r3), x3)
     send(*ex3)
     r3[mine, :] = s3[mine, :]
     loads["edget"].wait()
@@ -538,7 +527,7 @@
     for d in range(ng):
         s4[d] = (out_rows[:, 128 * d : 128 * d + 128] + sides[2 * kz * d : 2 * kz * (d + 1)]).reshape(2, kz, 128)
 
-    ex4 = ("grp", lambda d: s4.at[d], lambda d: r4.at[:, d], s4s, r4s)
+    ex4 = ("grp", lambda d: s4.at[d], lambda d: r4.at[:, d], r4.at[:, pl.ds(0, ng - 1)], x4)
     send(*ex4)
     r4[:, g] = s4[g]
     sent(*ex1)
@@ -575,17 +564,17 @@
 
     def backward(i, _):
         pair_x = jnp.concatenate([block[2 * i], block[2 * i + 1]], axis=1)
-        out = dot_left(sy[0], sy[1], pair_x)
+        out = dot_left(sy[...], pair_x)
         out = inverse_z(jnp.concatenate([out[:, :nz], out[:, nz:]], axis=0))
         grid[2 * i + 1, pl.ds(8, cy), :] = out[:cy]
         grid[2 * i + 2, pl.ds(8, cy), :] = out[cy:]
         return 0
 
-    lax.fori_loop(0, half, backward, 0)
+    lax.fori_loop(0, half, backward, 0, unroll=3)
     copy_out = pltpu.make_async_copy(grid.at[pl.ds(1, cx), pl.ds(8, cy), :], pot_h, osem)
     copy_out.start()
     pair_x = jnp.concatenate([solved[0, :cy], solved[1, :cy]], axis=1)
-    out = dot_left(sy[0], sy[1], pair_x)
+    out = dot_left(sy[...], pair_x)
     rest = jnp.concatenate([out[:, :nz], out[:, nz:], solved[0, cy:], solved[1, cy:]], axis=0)
     rest = inverse_z(rest)
     grid[0, pl.ds(8, cy), :] = rest[:cy]
@@ -637,9 +626,9 @@
             s6[pl.ds(pl.multiple_of(8 * d, 8), 8), :] = jnp.concatenate([mini] + slots, axis=0)
         return 0
 
-    lax.fori_loop(0, nf // some, gather, 0)
-
-    ex6 = ("fft", tile(s6), tile(r6), s6s, r6s)
+    lax.fori_loop(0, nf // some, gather, 0, unroll=2)
+
+    ex6 = ("fft", tile(s6), tile(r6), most_rows(r6), x6)
     send(*ex6)
     r6[mine, :] = s6[mine, :]
     sent(*ex4)
@@ -848,11 +837,7 @@
             vm((2 * nf, 8, 128)), vm((2 * nf, 8, 128)),
             vm((5, 8, 8, count)),
             dma((14,)), dma,
-            dma((ng,)), dma((ng,)),
-            dma((nf,)), dma((nf,)),
-            dma((nf,)), dma((nf,)),
-            dma((ng,)), dma((ng,)),
-            dma((nf,)), dma((nf,)),
+            dma((2,)), dma((2,)), dma((2,)), dma((2,)), dma((2,)),
         ],
         compiler_params=pltpu.CompilerParams(
             collective_id=0, has_side_effects=True, vmem_limit_bytes=limit

time: 65.6 us -> 56.8 us (0.87)
  Pallas kernels: 64.9 us -> 56.1 us
    pallas_call x1, Pallas kernels: 57.9 us -> 49 us  [root_call(): pl.pallas_call(functools.partial(root_kernel, (nf, ng, cx, cy, nz)), out_...]
where the time goes in v3:
time: 56.8 us; the launch traced here: 56.7 us
  Pallas kernels  56.1 us (99%)
  between operations  0.64 us (1%)
    pallas_call x1, Pallas kernels, root_call(): pl.pallas_call(functools.partial(root_kernel, (nf, ng, cx, cy, nz)), out_...  49 us
    pallas_call x1, Pallas kernels, root_call(): pl.pallas_call(patch_kernel, out_shape=(jax.ShapeDtypeStruct((8, 8, 8, co...  7.02 us

profile of v3, /device:TPU:1, one launch (start us, length us, event | category | flops | bytes accessed | tf_op | source)
XLA Modules:
  0.0 56.7 jit_solution(10177972624608992607)
XLA Ops:
  0.6 49.0 %shard_map.175 = (f32[24,96,128]{2,1,0:T(8,128)}, f32[256,128]{1,0:T(8,128)}, f32[8,128]{1,0:T(8,128)}, f32[5,8,8,8,32]{4,3,2,1,0:T(8,128)}) custom-call(s32[2,64]{1,0:T(2,128)} %bitcast.1, f32[24,96,128]{2,1,0:T(8,128)} %rho.1, f32[5,12,12,12,32]{4,3,2,1,0:T(8,128)} %fluid_h.3, bf16[256,256]{1,0:T(8,128)(2,1)} %constant.26.clone.sz_h, ...), custom_call_target="tpu_custom_call" | custom-call | tf_op jit(solution)/shard_map/pallas_call | solution.py:813
  49.7 7.0 %shard_map.176 = (f32[8,8,8,32]{3,2,1,0:T(8,128)}, f32[5,8,8,8,32]{4,3,2,1,0:T(8,128)}, f32[24,96,128]{2,1,0:T(8,128)}) custom-call(f32[256,128]{1,0:T(8,128)} %get-tuple-element.10.blocks, f32[8,128]{1,0:T(8,128)} %get-tuple-element.11.most, f32[5,8,8,8,32]{4,3,2,1,0:T(8,128)} %get-tuple-element.12.change_h, f32[5,12,12,12,32]{4,3,2,1,0:T(8,128)} %fluid_h.3, ...), custom_call_target="tpu_custom_call" | custom-call | tf_op jit(solution)/shard_map/pallas_call | solution.py:846

commit v4 on v3

--- a/solution.py
+++ b/solution.py
@@ -90,9 +90,10 @@
     column = np.broadcast_to(sy[0][:, None], (cy, 128))
     as32 = lambda t: np.ascontiguousarray(t, dtype=np.float32)
     szh, szl = halves(sz)
+    syh, syl = halves(sy)
     return dict(
         sz=np.block([[szh, szl], [szh, np.zeros_like(szh)]]).astype(ml_dtypes.bfloat16),
-        sy=np.concatenate(halves(sy)),
+        sy=np.block([[syh, syh], [syl, np.zeros_like(syl)]]).astype(ml_dtypes.bfloat16),
         sx=as32(sx),
         steps=as32(np.stack(steps)),
         wide=halves(wide.reshape(ng * 128, ny)),
@@ -122,26 +123,28 @@
 
 
 def dot_right(value, high, low):
+    rows = value.shape[0]
     a, b = split(value)
-    return mm(a, high) + (mm(b, high) + mm(a, low))
+    main = mm(jnp.concatenate([a, b], axis=0), high)
+    return main[:rows] + (main[rows:] + mm(a, low))
 
 
 def dot_left(both, value):
     rows = both.shape[0] // 2
     a, b = split(value)
-    main = mm(both, a)
-    return main[:rows] + (main[rows:] + mm(both[:rows], b))
+    out = mm(both, jnp.concatenate([a, b], axis=0))
+    return out[:rows] + out[rows:]
 
 
 def root_kernel(
     cfg,
     ghost, rho, fluid_h,
     sz_h, sy_h, sx_h, steps_h, wide_h, back_h, edge_h, edget_h, inv_h, pair_h, fold_h, column_h,
-    pot_h, blocks, most_out, change,
+    pot_h, blocks, most_out, packed_h,
     src, sz, sy, sx, steps, wide, back, edge, edget, inv, pair, fold, column, fluid, prim,
     block, solved, part, grid, hfield,
-    s1, r1, s2, r2, s3, r3, s4, r4, s6, r6, chain, mults, last_face,
-    tsem, osem, x1, x2, x3, x4, x6,
+    s1, r1, s2, r2, s3, r3, s4, r4, s6, r6, chain, mults, last_face, change, packed,
+    tsem, osem, psem, x1, x2, x3, x4, x6,
 ):
     nf, ng, cx, cy, nz = cfg
     kz = nz // ng
@@ -150,6 +153,22 @@
     f = lax.axis_index("fft")
     g = lax.axis_index("grp")
 
+    quarter = cx // 4
+    early = [
+        (f"rho{i}", rho.at[pl.ds(quarter * i, quarter)], src.at[pl.ds(quarter * i, quarter)]) for i in range(4)
+    ]
+    early[1:1] = [("sz", sz_h, sz), ("sy", sy_h, sy)]
+    early += [("steps", steps_h, steps), ("column", column_h, column), ("pair", pair_h.at[g, f], pair)]
+    late = [
+        ("wide", wide_h, wide), ("sx", sx_h, sx), ("edge", edge_h, edge), ("inv", inv_h.at[g], inv),
+        ("fluid", fluid_h, fluid), ("edget", edget_h, edget), ("back", back_h, back), ("fold", fold_h, fold),
+    ]
+    loads = {
+        name: pltpu.make_async_copy(a, b, tsem.at[i]) for i, (name, a, b) in enumerate(early + late)
+    }
+    for name, _, _ in early:
+        loads[name].start()
+
     ny_chips = 4 if nf % 4 == 0 else 1
     nz_chips = nf // ny_chips
     barrier = pltpu.get_barrier_semaphore()
@@ -179,21 +198,9 @@
     hello("fft")
     hello("grp")
 
-    loads = {}
-    order = [
-        ("rho", rho, src), ("sz", sz_h, sz), ("sy", sy_h, sy), ("steps", steps_h, steps),
-        ("column", column_h, column), ("pair", pair_h.at[g, f], pair), ("wide", wide_h, wide),
-        ("sx", sx_h, sx), ("edge", edge_h, edge), ("inv", inv_h.at[g], inv),
-        ("fluid", fluid_h, fluid), ("edget", edget_h, edget), ("back", back_h, back), ("fold", fold_h, fold),
-    ]
-    for i, (name, a, b) in enumerate(order):
-        loads[name] = pltpu.make_async_copy(a, b, tsem.at[i])
-        loads[name].start()
-
     sub = lax.broadcasted_iota(jnp.int32, (8, 128), 0)
     even = lax.rem(sub, 2) == 0
 
-    loads["rho"].wait()
     loads["sz"].wait()
     loads["sy"].wait()
 
@@ -208,7 +215,12 @@
         block[2 * i + 1] = out[:, nz:]
         return 0
 
-    lax.fori_loop(0, half, forward, 0, unroll=3)
+    for part_of in range(4):
+        loads[f"rho{part_of}"].wait()
+        if part_of == 3:
+            for name, _, _ in late:
+                loads[name].start()
+        lax.fori_loop(part_of * half // 4, (part_of + 1) * half // 4, forward, 0, unroll=True)
 
     loads["steps"].wait()
     loads["column"].wait()
@@ -439,7 +451,7 @@
     zero = jnp.zeros((kz, wide_lane), F32)
     sums = [jnp.zeros((kz, ny), F32), jnp.zeros((kz, ny), F32)]
     first_row = [float(v) for v in sine(cx)[0]]
-    group = 4
+    group = cx // 2
     for x0 in range(0, cx, group):
         lhs = jnp.concatenate(
             [jnp.where(diag, jnp.broadcast_to(edge_k[x : x + 1], (kz, wide_lane)), zero) for x in range(x0, x0 + group)],
@@ -570,7 +582,7 @@
         grid[2 * i + 2, pl.ds(8, cy), :] = out[cy:]
         return 0
 
-    lax.fori_loop(0, half, backward, 0, unroll=3)
+    lax.fori_loop(0, half, backward, 0, unroll=True)
     copy_out = pltpu.make_async_copy(grid.at[pl.ds(1, cx), pl.ds(8, cy), :], pot_h, osem)
     copy_out.start()
     pair_x = jnp.concatenate([solved[0, :cy], solved[1, :cy]], axis=1)
@@ -631,29 +643,49 @@
     ex6 = ("fft", tile(s6), tile(r6), most_rows(r6), x6)
     send(*ex6)
     r6[mine, :] = s6[mine, :]
+    width = fluid.shape[-1]
+    groups = 128 // width
+    rate = COURANT / most_out[pl.ds(0, 1), pl.ds(0, width)]
+
+    def pack(y, _):
+        for r in range(2):
+            at = [2 * i + r for i in range(groups)]
+            cons = [[fluid[v, x + 2, y + 2, cells, :] for x in at] for v in range(5)]
+            for v in range(4):
+                packed[v, r, y] = jnp.concatenate(cons[v], axis=1)
+            for v in range(5):
+                packed[4 + v, r, y] = jnp.concatenate(
+                    [c - rate * change[v, x, y] for c, x in zip(cons[v], at)], axis=1
+                )
+        return 0
+
+    lax.fori_loop(0, 8, pack, 0)
+    copy_packed = pltpu.make_async_copy(packed, packed_h, psem)
+    copy_packed.start()
     sent(*ex4)
     copy_out.wait()
+    copy_packed.wait()
     receive(*ex6)
     blocks[...] = r6[...]
     sent(*ex6)
 
 
 def patch_kernel(
-    blocks, most, change_h, fluid_h, pot_in, weave,
-    fine, moved, pot_out,
-    fluid, change, force, state, hold, sems,
+    blocks, most, packed_h, pot_in, weave,
+    fine_h, moved_h, pot_out,
+    fine, moved, packed, hold, sems,
 ):
     count = fine.shape[-1]
     nf = blocks.shape[0] // 8
-    copies = [
-        pltpu.make_async_copy(fluid_h.at[0], fluid.at[0], sems.at[0]),
-        pltpu.make_async_copy(pot_in, hold, sems.at[1]),
-        pltpu.make_async_copy(change_h, change, sems.at[2]),
-        pltpu.make_async_copy(fluid_h.at[pl.ds(1, 4)], fluid.at[pl.ds(1, 4)], sems.at[3]),
+    copy_in = pltpu.make_async_copy(pot_in, hold, sems.at[0])
+    needs = [
+        pltpu.make_async_copy(packed_h.at[0], packed.at[0], sems.at[8]),
+        pltpu.make_async_copy(packed_h.at[pl.ds(1, 8)], packed.at[pl.ds(1, 8)], sems.at[9]),
     ]
-    for c in copies:
-        c.start()
-    copy_out = pltpu.make_async_copy(hold, pot_out, sems.at[4])
+    needs[0].start()
+    copy_in.start()
+    needs[1].start()
+    copy_out = pltpu.make_async_copy(hold, pot_out, sems.at[1])
     groups = 128 // count
 
     lanes = lax.rem(lax.broadcasted_iota(jnp.int32, (nf, 128), 1), count)
@@ -700,16 +732,14 @@
             else 0.25 * values[low] + 0.75 * values[low + 1]
         )
 
-    copies[0].wait()
     scale = 1.0 / (6.0 + SCREEN * FINE_STEP * FINE_STEP)
-    layers = {}
-    rims = {}
+    layers, rims, states, force = {}, {}, {}, {}
     for r in range(2):
         plane = [along_x(within, r, y) for y in range(6)]
         for jy in range(10):
             value = between(plane, jy)
             if 1 <= jy <= 8:
-                state[r, jy - 1] = value
+                states[r, jy - 1] = value
             else:
                 rims[r, jy] = value
         plane = [along_x(outside, r, y) for y in range(6)]
@@ -719,79 +749,91 @@
         [0.75 * within[0][y] + 0.25 * within[1][y] for y in range(6)],
         [0.25 * within[4][y] + 0.75 * within[5][y] for y in range(6)],
     )
-    for r in range(2):
-        for y in range(8):
-            rho = jnp.concatenate(
-                [fluid[0, 2 * i + r + 2, y + 2, pl.ds(2, 8), :] for i in range(groups)], axis=1
-            )
-            side = jnp.where(first if r == 0 else final, between(ends[r], y + 1), 0.0)
-            ghost = layers[r, y] + side
-            if y == 0:
-                ghost = ghost + rims[r, 0]
-            if y == 7:
-                ghost = ghost + rims[r, 9]
-            force[r, y] = (OMEGA * scale) * (ghost - FINE_STEP * FINE_STEP * rho)
-
-    copies[1].wait()
+    keys = [(r, y) for r in range(2) for y in range(8)]
+    sides = {
+        (r, y): jnp.where(first if r == 0 else final, between(ends[r], y + 1), 0.0) for r, y in keys
+    }
+    needs[0].wait()
+    for r, y in keys:
+        ghost = layers[r, y] + sides[r, y]
+        if y == 0:
+            ghost = ghost + rims[r, 0]
+        if y == 7:
+            ghost = ghost + rims[r, 9]
+        force[r, y] = (OMEGA * scale) * (ghost - FINE_STEP * FINE_STEP * packed[0, r, y])
+
+    copy_in.wait()
     copy_out.start()
 
-    def beside(r, y, v):
-        other = state[1 - r, y]
+    def beside(old, r, y):
+        other = old[1 - r, y]
         if r == 0:
-            far = jnp.where(first, 0.0, pltpu.roll(other, count, 1))
-        else:
-            far = jnp.where(final, 0.0, pltpu.roll(other, 128 - count, 1))
-        return other, far
+            return other, jnp.where(first, 0.0, pltpu.roll(other, count, 1))
+        return other, jnp.where(final, 0.0, pltpu.roll(other, 128 - count, 1))
 
     def sweep(_, carry):
+        old = dict(zip(keys, carry))
         for colour in (0, 1):
-            for r in range(2):
-                for y in range(8):
-                    v = state[r, y]
-                    other, far = beside(r, y, v)
-                    near = (other + far) + (
-                        jnp.where(bottom, 0.0, pltpu.roll(v, 1, 0)) + jnp.where(top, 0.0, pltpu.roll(v, 7, 0))
-                    )
-                    if y > 0:
-                        near = near + state[r, y - 1]
-                    if y < 7:
-                        near = near + state[r, y + 1]
-                    new = (1.0 - OMEGA) * v + ((OMEGA * scale) * near + force[r, y])
-                    mask = zeven if (r + y + colour) % 2 == 0 else zodd
-                    state[r, y] = jnp.where(mask, new, v)
-        return carry
-
-    lax.fori_loop(0, SWEEPS, sweep, 0)
-
-    copies[2].wait()
-    copies[3].wait()
-    step = COURANT * FINE_STEP / most[pl.ds(0, 1), pl.ds(0, count)]
-    rate = step / FINE_STEP
-    for r in range(2):
-        for y in range(8):
-            v = state[r, y]
-            other, far = beside(r, y, v)
-            far = far + jnp.where(first if r == 0 else final, between(ends[r], y + 1), 0.0)
-            layer = layers[r, y]
-            down = state[r, y - 1] if y > 0 else rims[r, 0]
-            up = state[r, y + 1] if y < 7 else rims[r, 9]
-            pull = (
-                far - other if r == 0 else other - far,
-                down - up,
-                jnp.where(bottom, layer, pltpu.roll(v, 1, 0)) - jnp.where(top, layer, pltpu.roll(v, 7, 0)),
-            )
-            for i in range(groups):
-                x = 2 * i + r
-                at = slice(count * i, count * (i + 1))
-                fine[x, y] = v[:, at]
-                cons = [fluid[k, x + 2, y + 2, pl.ds(2, 8), :] for k in range(5)]
-                work = 0.0
-                moved[0, x, y] = cons[0] - rate * change[0, x, y]
-                for n in range(3):
-                    force_n = pull[n][:, at]
-                    moved[1 + n, x, y] = cons[1 + n] - rate * change[1 + n, x, y] + step * cons[0] * force_n
-                    work = work + cons[1 + n] * force_n
-                moved[4, x, y] = cons[4] - rate * change[4, x, y] + step * work
+            new = {}
+            for r, y in keys:
+                v = old[r, y]
+                other, far = beside(old, r, y)
+                near = (other + far) + (
+                    jnp.where(bottom, 0.0, pltpu.roll(v, 1, 0)) + jnp.where(top, 0.0, pltpu.roll(v, 7, 0))
+                )
+                if y > 0:
+                    near = near + old[r, y - 1]
+                if y < 7:
+                    near = near + old[r, y + 1]
+                value = (1.0 - OMEGA) * v + ((OMEGA * scale) * near + force[r, y])
+                mask = zeven if (r + y + colour) % 2 == 0 else zodd
+                new[r, y] = jnp.where(mask, value, v)
+            old = new
+        return tuple(old[k] for k in keys)
+
+    out = lax.fori_loop(0, SWEEPS, sweep, tuple(states[k] for k in keys))
+    states = dict(zip(keys, out))
+
+    def spill(target, r, y, value):
+        for i in range(groups):
+            target[2 * i + r, y] = value[:, count * i : count * (i + 1)]
+
+    copies = [pltpu.make_async_copy(fine, fine_h, sems.at[2])] + [
+        pltpu.make_async_copy(moved.at[v], moved_h.at[v], sems.at[3 + v]) for v in range(5)
+    ]
+    for r, y in keys:
+        spill(fine, r, y, states[r, y])
+    copies[0].start()
+
+    needs[1].wait()
+    for r, y in keys:
+        spill(moved.at[0], r, y, packed[4, r, y])
+    copies[1].start()
+    step = COURANT * FINE_STEP / most[pl.ds(0, 1), :]
+    work = {}
+    for n in range(3):
+        for r, y in keys:
+            v = states[r, y]
+            if n == 0:
+                other, far = beside(states, r, y)
+                far = far + sides[r, y]
+                pull = far - other if r == 0 else other - far
+            elif n == 1:
+                down = states[r, y - 1] if y > 0 else rims[r, 0]
+                up = states[r, y + 1] if y < 7 else rims[r, 9]
+                pull = down - up
+            else:
+                layer = layers[r, y]
+                pull = jnp.where(bottom, layer, pltpu.roll(v, 1, 0)) - jnp.where(top, layer, pltpu.roll(v, 7, 0))
+            spill(moved.at[1 + n], r, y, packed[5 + n, r, y] + step * packed[0, r, y] * pull)
+            part = packed[1 + n, r, y] * pull
+            work[r, y] = part if n == 0 else work[r, y] + part
+        copies[2 + n].start()
+    for r, y in keys:
+        spill(moved.at[4], r, y, packed[8, r, y] + step * work[r, y])
+    copies[5].start()
+    for c in copies:
+        c.wait()
     copy_out.wait()
 
 
@@ -810,16 +852,16 @@
     local["inv"] = local["inv"][1:]
     local["pair"] = local["pair"][2:]
     limit = 56 * 1024 * 1024
-    potential, blocks, most, change = pl.pallas_call(
+    potential, blocks, most, packed = pl.pallas_call(
         functools.partial(root_kernel, (nf, ng, cx, cy, nz)),
         out_shape=(
             jax.ShapeDtypeStruct((cx, cy, nz), F32),
             jax.ShapeDtypeStruct((nf * 8, 128), F32),
             jax.ShapeDtypeStruct((8, 128), F32),
-            jax.ShapeDtypeStruct((5, 8, 8, 8, count), F32),
+            jax.ShapeDtypeStruct((9, 2, 8, 8, 128), F32),
         ),
         in_specs=[pl.BlockSpec(memory_space=pltpu.SMEM)] + [anyspace] * (2 + len(NAMES)),
-        out_specs=(anyspace, vspace, vspace, vspace),
+        out_specs=(anyspace, vspace, vspace, anyspace),
         scratch_shapes=[vm((cx, cy, nz))]
         + [vm(local[n], consts[i].dtype) for i, n in enumerate(NAMES)]
         + [
@@ -836,7 +878,8 @@
             vm((nf * 8, 128)), vm((nf * 8, 128)),
             vm((2 * nf, 8, 128)), vm((2 * nf, 8, 128)),
             vm((5, 8, 8, count)),
-            dma((14,)), dma,
+            vm((5, 8, 8, 8, count)), vm((9, 2, 8, 8, 128)),
+            dma((17,)), dma, dma,
             dma((2,)), dma((2,)), dma((2,)), dma((2,)), dma((2,)),
         ],
         compiler_params=pltpu.CompilerParams(
@@ -850,15 +893,13 @@
             jax.ShapeDtypeStruct((5, 8, 8, 8, count), F32),
             jax.ShapeDtypeStruct((cx, cy, nz), F32),
         ),
-        in_specs=[vspace, vspace, anyspace, anyspace, anyspace, vspace],
-        out_specs=(vspace, vspace, anyspace),
+        in_specs=[vspace, vspace, anyspace, anyspace, vspace],
+        out_specs=(anyspace, anyspace, anyspace),
         scratch_shapes=[
-            vm(fluid.shape), vm((5, 8, 8, 8, count)),
-            vm((2, 8, 8, 128)), vm((2, 8, 8, 128)), vm((cx, cy, nz)),
-            dma((5,)),
+            vm((8, 8, 8, count)), vm((5, 8, 8, 8, count)), vm((9, 2, 8, 8, 128)), vm((cx, cy, nz)), dma((10,)),
         ],
         compiler_params=pltpu.CompilerParams(vmem_limit_bytes=limit),
-    )(blocks, most, change, fluid, potential, jnp.asarray(tab["weave"]))
+    )(blocks, most, packed, potential, jnp.asarray(tab["weave"]))
     return potential, fine, moved
 
 

time: 56.8 us -> 50.4 us (0.89)
  Pallas kernels: 56.1 us -> 49.6 us
    pallas_call x1, Pallas kernels: 49 us -> 44.5 us  [root_call(): pl.pallas_call(functools.partial(root_kernel, (nf, ng, cx, cy, nz)), out_...]
    pallas_call x1, Pallas kernels: 7.02 us -> 5.06 us  [root_call(): pl.pallas_call(patch_kernel, out_shape=(jax.ShapeDtypeStruct((8, 8, 8, co...]
where the time goes in v4:
time: 50.4 us; the launch traced here: 50.2 us
  Pallas kernels  49.6 us (98%)
  between operations  0.64 us (1%)
    pallas_call x1, Pallas kernels, root_call(): pl.pallas_call(functools.partial(root_kernel, (nf, ng, cx, cy, nz)), out_...  44.5 us
    pallas_call x1, Pallas kernels, root_call(): pl.pallas_call(patch_kernel, out_shape=(jax.ShapeDtypeStruct((8, 8, 8, co...  5.06 us

profile of v4, /device:TPU:1, one launch (start us, length us, event | category | flops | bytes accessed | tf_op | source)
XLA Modules:
  0.0 50.2 jit_solution(5028843340318884771)
XLA Ops:
  0.6 44.5 %shard_map.175 = (f32[24,96,128]{2,1,0:T(8,128)}, f32[256,128]{1,0:T(8,128)}, f32[8,128]{1,0:T(8,128)}, f32[9,2,8,8,128]{4,3,2,1,0:T(8,128)}) custom-call(s32[2,64]{1,0:T(2,128)} %bitcast.1, f32[24,96,128]{2,1,0:T(8,128)} %rho.1, f32[5,12,12,12,32]{4,3,2,1,0:T(8,128)} %fluid_h.1, bf16[256,256]{1,0:T(8,128)(2,1)} %constant.26.clone.sz_h, ...), custom_call_target="tpu_custom_call" | custom-call | tf_op jit(solution)/shard_map/pallas_call | solution.py:855
  45.2 5.1 %shard_map.176 = (f32[8,8,8,32]{3,2,1,0:T(8,128)}, f32[5,8,8,8,32]{4,3,2,1,0:T(8,128)}, f32[24,96,128]{2,1,0:T(8,128)}) custom-call(f32[256,128]{1,0:T(8,128)} %get-tuple-element.10.blocks, f32[8,128]{1,0:T(8,128)} %get-tuple-element.11.most, f32[9,2,8,8,128]{4,3,2,1,0:T(8,128)} %get-tuple-element.12.packed_h, f32[24,96,128]{2,1,0:T(8,128)} %get-tuple-element.13.pot_in, ...), custom_call_target="tpu_custom_call" | custom-call | tf_op jit(solution)/shard_map/pallas_call | solution.py:889

commit v5 on v4

--- a/solution.py
+++ b/solution.py
@@ -91,10 +91,18 @@
     as32 = lambda t: np.ascontiguousarray(t, dtype=np.float32)
     szh, szl = halves(sz)
     syh, syl = halves(sy)
+    wide_x = np.zeros((cx, 32))
+    wide_x[:, :cx] = sx
+    xh, xl = halves(np.repeat(wide_x, kz, axis=0))
+    sx_rows = np.block([[xh, xh], [xl, np.zeros_like(xl)]]).astype(ml_dtypes.bfloat16)
+    tall_x = np.zeros((32, cx * kz))
+    tall_x[:cx] = np.repeat(sx, kz, axis=1)
+    sx_sums = np.concatenate(halves(tall_x))
     return dict(
         sz=np.block([[szh, szl], [szh, np.zeros_like(szh)]]).astype(ml_dtypes.bfloat16),
         sy=np.block([[syh, syh], [syl, np.zeros_like(syl)]]).astype(ml_dtypes.bfloat16),
-        sx=as32(sx),
+        sx=sx_rows,
+        sxt=sx_sums,
         steps=as32(np.stack(steps)),
         wide=halves(wide.reshape(ng * 128, ny)),
         back=halves(np.ascontiguousarray(back.reshape(ng * 128, ny).T)),
@@ -109,7 +117,7 @@
 
 
 NAMES = (
-    "sz", "sy", "sx", "steps", "wide", "back", "edge", "edget", "inv", "pair", "fold", "column",
+    "sz", "sy", "sx", "sxt", "steps", "wide", "back", "edge", "edget", "inv", "pair", "fold", "column",
 )
 
 
@@ -139,9 +147,9 @@
 def root_kernel(
     cfg,
     ghost, rho, fluid_h,
-    sz_h, sy_h, sx_h, steps_h, wide_h, back_h, edge_h, edget_h, inv_h, pair_h, fold_h, column_h,
+    sz_h, sy_h, sx_h, sxt_h, steps_h, wide_h, back_h, edge_h, edget_h, inv_h, pair_h, fold_h, column_h,
     pot_h, blocks, most_out, packed_h,
-    src, sz, sy, sx, steps, wide, back, edge, edget, inv, pair, fold, column, fluid, prim,
+    src, sz, sy, sx, sxt, steps, wide, back, edge, edget, inv, pair, fold, column, fluid, prim,
     block, solved, part, grid, hfield,
     s1, r1, s2, r2, s3, r3, s4, r4, s6, r6, chain, mults, last_face, change, packed,
     tsem, osem, psem, x1, x2, x3, x4, x6,
@@ -161,7 +169,7 @@
     early += [("steps", steps_h, steps), ("column", column_h, column), ("pair", pair_h.at[g, f], pair)]
     late = [
         ("wide", wide_h, wide), ("sx", sx_h, sx), ("edge", edge_h, edge), ("inv", inv_h.at[g], inv),
-        ("fluid", fluid_h, fluid), ("edget", edget_h, edget), ("back", back_h, back), ("fold", fold_h, fold),
+        ("fluid", fluid_h, fluid), ("edget", edget_h, edget), ("sxt", sxt_h, sxt), ("back", back_h, back), ("fold", fold_h, fold),
     ]
     loads = {
         name: pltpu.make_async_copy(a, b, tsem.at[i]) for i, (name, a, b) in enumerate(early + late)
@@ -259,7 +267,7 @@
         solved[1, at, :] = values[cx - 1]
         return 0
 
-    lax.fori_loop(0, cy // 16, first, 0)
+    lax.fori_loop(0, cy // 16, first, 0, unroll=2)
     sums = part[...]
     sign = jnp.where(even, 1.0, -1.0)
     edges = (jnp.sum(sums, axis=1), jnp.sum(sums * sign[None], axis=1))
@@ -428,7 +436,7 @@
         mults[2 * i + 1] = m1
         return m1
 
-    lax.fori_loop(0, nf, coefficients, jnp.zeros((8, 128), F32))
+    lax.fori_loop(0, nf // 2, coefficients, jnp.zeros((8, 128), F32))
     loads["fluid"].wait()
     lax.fori_loop(0, 12, make_cells, 0)
     most = jnp.full((1, 128), top_speed(), F32)
@@ -442,21 +450,17 @@
     main = dot_right(main, wide[0], wide[1])
     across = r1[...].reshape(ng * 2 * kz, 128).T
     edge_x = across[cy : cy + cx]
-    edge_k = jnp.dot(sx[...], edge_x, precision=lax.Precision.HIGHEST, preferred_element_type=F32)
+    edge_k = dot_left(sx[...], across[cy : cy + 32]).reshape(cx, kz, ng * 2 * kz)
     wide_lane = ng * 2 * kz
     diag = (
         lax.rem(lax.broadcasted_iota(jnp.int32, (kz, wide_lane), 1), kz)
         == lax.broadcasted_iota(jnp.int32, (kz, wide_lane), 0)
     )
-    zero = jnp.zeros((kz, wide_lane), F32)
     sums = [jnp.zeros((kz, ny), F32), jnp.zeros((kz, ny), F32)]
     first_row = [float(v) for v in sine(cx)[0]]
     group = cx // 2
     for x0 in range(0, cx, group):
-        lhs = jnp.concatenate(
-            [jnp.where(diag, jnp.broadcast_to(edge_k[x : x + 1], (kz, wide_lane)), zero) for x in range(x0, x0 + group)],
-            axis=0,
-        )
+        lhs = jnp.where(diag[None], edge_k[x0 : x0 + group], 0.0).reshape(group * kz, wide_lane)
         out = dot_right(lhs, edge[0], edge[1])
         for x in range(x0, x0 + group):
             hd = out[(x - x0) * kz : (x - x0 + 1) * kz] * inv[x]
@@ -481,19 +485,38 @@
     most = jnp.max(r2[pl.ds(6, nf, stride=8), :], axis=0, keepdims=True)
 
     last = jnp.zeros((8, 128), F32)
-    prev = last
-    for d in range(nf):
+
+    def right_sides(d):
         msg = r2[8 * d : 8 * d + 8, :]
         other = pltpu.roll(msg, 5, 0)
+        return msg - cb * other, other - cb * msg
+
+    up = down = last
+    for d in range(nf // 2):
         m0, m1 = mults[2 * d], mults[2 * d + 1]
-        prev = m0 * (msg - cb * other) + (m0 * ca) * prev
-        chain[2 * d] = prev
-        prev = m1 * (other - cb * msg) + (m1 * cb) * prev
-        chain[2 * d + 1] = prev
-    chain[2 * nf - 1] = prev
-    for j in range(2 * nf - 2, -1, -1):
-        prev = chain[j] + (mults[j] * (cb if j % 2 == 0 else ca)) * prev
-        chain[j] = prev
+        ma, mb = m0 * ca, m1 * cb
+        e = nf - 1 - d
+        p, q = right_sides(d)
+        up = m0 * p + ma * up
+        chain[2 * d] = up
+        up = m1 * q + mb * up
+        chain[2 * d + 1] = up
+        p, q = right_sides(e)
+        down = m0 * q + ma * down
+        chain[2 * e + 1] = down
+        down = m1 * p + mb * down
+        chain[2 * e] = down
+    link = mults[nf - 1] * ca
+    over = 1.0 / (1.0 - link * link)
+    up, down = (up + link * down) * over, (down + link * up) * over
+    chain[nf - 1] = up
+    chain[nf] = down
+    for j in range(nf - 2, -1, -1):
+        m = mults[j] * (cb if j % 2 == 0 else ca)
+        up = chain[j] + m * up
+        chain[j] = up
+        down = chain[2 * nf - 1 - j] + m * down
+        chain[2 * nf - 1 - j] = down
     for d in range(nf):
         left = chain[2 * d - 1] if d > 0 else last
         right = chain[2 * d + 2] if d < nf - 1 else last
@@ -521,10 +544,11 @@
             [hfield[x] + (first_row[x] * inv[x]) * mixed[x % 2] for x in range(x0, x0 + group)], axis=0
         )
         out = dot_right(lhs, edget[0], edget[1])
-        for x in range(group):
-            corr.append(jnp.sum(jnp.where(diag, out[x * kz : (x + 1) * kz], zero), axis=0, keepdims=True))
-    corr = jnp.concatenate(corr, axis=0)
-    corr = jnp.dot(sx[...], corr, precision=lax.Precision.HIGHEST, preferred_element_type=F32)
+        corr.append(jnp.where(diag[None], out.reshape(group, kz, wide_lane), 0.0).reshape(group * kz, wide_lane))
+    loads["sxt"].wait()
+    a, b = split(jnp.concatenate(corr, axis=0))
+    main = mm(sxt[...], a)
+    corr = (main[:32] + (main[32:] + mm(sxt[pl.ds(0, 32), :], b)))[:cx]
     blank = jnp.zeros((cx, kz), F32)
     from_left = jnp.concatenate([blank, edge_x[:, :-kz]], axis=1)
     from_right = jnp.concatenate([edge_x[:, kz:], blank], axis=1)
@@ -550,11 +574,14 @@
         solved[e] = r4[e].reshape(nz, 128).T
     most_out[...] = jnp.full((8, 128), jnp.max(solved[0, pl.ds(127, 1), :]), F32)
 
+    for x in range(cx):
+        va = solved[0, pl.ds(cy + x, 1), :]
+        vb = solved[1, pl.ds(cy + x, 1), :]
+        part[x] = jnp.where(even, va + vb, va - vb)
+
     def second_solve(i, _):
         def fetch(x, at):
-            va = solved[0, pl.ds(cy + x, 1), :]
-            vb = solved[1, pl.ds(cy + x, 1), :]
-            w = jnp.where(even, va + vb, va - vb)
+            w = part[x]
             value = block[x, at, :] - column[at, :] * jnp.concatenate([w, w], axis=0)
             if x == 0:
                 value = value - solved[0, at, :]
@@ -567,7 +594,7 @@
             block[x, at, :] = values[x]
         return 0
 
-    lax.fori_loop(0, cy // 16, second_solve, 0)
+    lax.fori_loop(0, cy // 16, second_solve, 0, unroll=2)
 
     def inverse_z(rows):
         a, b = split(rows)
@@ -876,10 +903,10 @@
             vm((nf * 8, 128)), vm((nf * 8, 128)),
             vm((ng, 2, kz, 128)), vm((2, ng, kz, 128)),
             vm((nf * 8, 128)), vm((nf * 8, 128)),
-            vm((2 * nf, 8, 128)), vm((2 * nf, 8, 128)),
+            vm((2 * nf, 8, 128)), vm((nf, 8, 128)),
             vm((5, 8, 8, count)),
             vm((5, 8, 8, 8, count)), vm((9, 2, 8, 8, 128)),
-            dma((17,)), dma, dma,
+            dma((18,)), dma, dma,
             dma((2,)), dma((2,)), dma((2,)), dma((2,)), dma((2,)),
         ],
         compiler_params=pltpu.CompilerParams(

time: 50.4 us -> 50 us (level)
  no operation moved by 1% of the time
where the time goes in v5:
time: 50 us; the launch traced here: 49.8 us
  Pallas kernels  49.2 us (98%)
  between operations  0.64 us (1%)
    pallas_call x1, Pallas kernels, root_call(): pl.pallas_call(functools.partial(root_kernel, (nf, ng, cx, cy, nz)), out_...  44.1 us
    pallas_call x1, Pallas kernels, root_call(): pl.pallas_call(patch_kernel, out_shape=(jax.ShapeDtypeStruct((8, 8, 8, co...  5.06 us

profile of v5, /device:TPU:1, one launch (start us, length us, event | category | flops | bytes accessed | tf_op | source)
XLA Modules:
  0.0 49.8 jit_solution(2543112107201738246)
XLA Ops:
  0.6 44.1 %shard_map.184 = (f32[24,96,128]{2,1,0:T(8,128)}, f32[256,128]{1,0:T(8,128)}, f32[8,128]{1,0:T(8,128)}, f32[9,2,8,8,128]{4,3,2,1,0:T(8,128)}) custom-call(s32[2,64]{1,0:T(2,128)} %bitcast.1, f32[24,96,128]{2,1,0:T(8,128)} %rho.1, f32[5,12,12,12,32]{4,3,2,1,0:T(8,128)} %fluid_h.1, bf16[256,256]{1,0:T(8,128)(2,1)} %constant.28.clone.sz_h, ...), custom_call_target="tpu_custom_call" | custom-call | tf_op jit(solution)/shard_map/pallas_call | solution.py:882
  44.7 5.1 %shard_map.185 = (f32[8,8,8,32]{3,2,1,0:T(8,128)}, f32[5,8,8,8,32]{4,3,2,1,0:T(8,128)}, f32[24,96,128]{2,1,0:T(8,128)}) custom-call(f32[256,128]{1,0:T(8,128)} %get-tuple-element.10.blocks, f32[8,128]{1,0:T(8,128)} %get-tuple-element.11.most, f32[9,2,8,8,128]{4,3,2,1,0:T(8,128)} %get-tuple-element.12.packed_h, f32[24,96,128]{2,1,0:T(8,128)} %get-tuple-element.13.pot_in, ...), custom_call_target="tpu_custom_call" | custom-call | tf_op jit(solution)/shard_map/pallas_call | solution.py:916

commit v6 on v5

--- a/solution.py
+++ b/solution.py
@@ -110,7 +110,7 @@
         edget=halves(np.ascontiguousarray(repeated.T)),
         inv=as32(1.0 / denom),
         pair=as32(pair),
-        weave=weave.astype(ml_dtypes.bfloat16),
+        weave=np.concatenate([weave, weave], axis=1).astype(ml_dtypes.bfloat16),
         fold=np.concatenate([fold, fold]).astype(ml_dtypes.bfloat16),
         column=as32(column),
     )
@@ -148,11 +148,11 @@
     cfg,
     ghost, rho, fluid_h,
     sz_h, sy_h, sx_h, sxt_h, steps_h, wide_h, back_h, edge_h, edget_h, inv_h, pair_h, fold_h, column_h,
-    pot_h, blocks, most_out, packed_h,
+    pot_h, blocks_h, most_h, packed_h,
     src, sz, sy, sx, sxt, steps, wide, back, edge, edget, inv, pair, fold, column, fluid, prim,
     block, solved, part, grid, hfield,
-    s1, r1, s2, r2, s3, r3, s4, r4, s6, r6, chain, mults, last_face, change, packed,
-    tsem, osem, psem, x1, x2, x3, x4, x6,
+    s1, r1, s2, r2, s3, r3, s4, r4, s6, most_out, chain, mults, last_face, change, packed,
+    tsem, osem, psem, bsem, msem, x1, x2, x3, x4, x6,
 ):
     nf, ng, cx, cy, nz = cfg
     kz = nz // ng
@@ -573,6 +573,8 @@
     for e in range(2):
         solved[e] = r4[e].reshape(nz, 128).T
     most_out[...] = jnp.full((8, 128), jnp.max(solved[0, pl.ds(127, 1), :]), F32)
+    copy_most = pltpu.make_async_copy(most_out, most_h, msem)
+    copy_most.start()
 
     for x in range(cx):
         va = solved[0, pl.ds(cy + x, 1), :]
@@ -667,9 +669,10 @@
 
     lax.fori_loop(0, nf // some, gather, 0, unroll=2)
 
-    ex6 = ("fft", tile(s6), tile(r6), most_rows(r6), x6)
+    ex6 = ("fft", tile(s6), tile(blocks_h), most_rows(blocks_h), x6)
     send(*ex6)
-    r6[mine, :] = s6[mine, :]
+    copy_mine = pltpu.make_async_copy(s6.at[mine, :], blocks_h.at[mine, :], bsem)
+    copy_mine.start()
     width = fluid.shape[-1]
     groups = 128 // width
     rate = COURANT / most_out[pl.ds(0, 1), pl.ds(0, width)]
@@ -692,9 +695,10 @@
     sent(*ex4)
     copy_out.wait()
     copy_packed.wait()
+    copy_most.wait()
+    copy_mine.wait()
+    sent(*ex6)
     receive(*ex6)
-    blocks[...] = r6[...]
-    sent(*ex6)
 
 
 def patch_kernel(
@@ -719,17 +723,15 @@
     hot = jnp.concatenate(
         [
             jnp.where(blocks[pl.ds(6 + c, nf, stride=8), :] == lanes.astype(F32), 1.0, 0.0)
-            for c in range(2)
+            for c in (0, 1, 0, 1)
         ],
         axis=0,
     ).astype(BF16)
     within, outside = [], []
     for t in range(3):
         came = jnp.concatenate([blocks[pl.ds(c * 3 + t, nf, stride=8), :] for c in range(2)], axis=0)
-        a, b = split(came.T)
-        placed = mm(a, hot) + mm(b, hot)
-        a, b = split(placed)
-        woven = mm(weave[...], a) + mm(weave[...], b)
+        placed = mm(jnp.concatenate(split(came.T), axis=1), hot)
+        woven = mm(weave[...], jnp.concatenate(split(placed), axis=0))
         woven = woven.reshape(2, 2, 8, 8, 128)
         within += [woven[0, 0], woven[0, 1]]
         outside += [woven[1, 0], woven[1, 1]]
@@ -798,21 +800,28 @@
             return other, jnp.where(first, 0.0, pltpu.roll(other, count, 1))
         return other, jnp.where(final, 0.0, pltpu.roll(other, 128 - count, 1))
 
+    weight = OMEGA * scale
+    from_below = jnp.where(bottom, 0.0, weight)
+    from_above = jnp.where(top, 0.0, weight)
+    from_left = jnp.where(first, 0.0, weight)
+    from_right = jnp.where(final, 0.0, weight)
+
     def sweep(_, carry):
         old = dict(zip(keys, carry))
         for colour in (0, 1):
             new = {}
             for r, y in keys:
                 v = old[r, y]
-                other, far = beside(old, r, y)
-                near = (other + far) + (
-                    jnp.where(bottom, 0.0, pltpu.roll(v, 1, 0)) + jnp.where(top, 0.0, pltpu.roll(v, 7, 0))
-                )
+                other = old[1 - r, y]
+                far = pltpu.roll(other, count if r == 0 else 128 - count, 1)
+                near = other
                 if y > 0:
                     near = near + old[r, y - 1]
                 if y < 7:
                     near = near + old[r, y + 1]
-                value = (1.0 - OMEGA) * v + ((OMEGA * scale) * near + force[r, y])
+                value = ((1.0 - OMEGA) * v + force[r, y]) + weight * near
+                value = value + (from_below * pltpu.roll(v, 1, 0) + from_above * pltpu.roll(v, 7, 0))
+                value = value + (from_left if r == 0 else from_right) * far
                 mask = zeven if (r + y + colour) % 2 == 0 else zodd
                 new[r, y] = jnp.where(mask, value, v)
             old = new
@@ -888,7 +897,7 @@
             jax.ShapeDtypeStruct((9, 2, 8, 8, 128), F32),
         ),
         in_specs=[pl.BlockSpec(memory_space=pltpu.SMEM)] + [anyspace] * (2 + len(NAMES)),
-        out_specs=(anyspace, vspace, vspace, anyspace),
+        out_specs=(anyspace,) * 4,
         scratch_shapes=[vm((cx, cy, nz))]
         + [vm(local[n], consts[i].dtype) for i, n in enumerate(NAMES)]
         + [
@@ -902,11 +911,11 @@
             vm((nf * 8, 128)), vm((nf * 8, 128)),
             vm((nf * 8, 128)), vm((nf * 8, 128)),
             vm((ng, 2, kz, 128)), vm((2, ng, kz, 128)),
-            vm((nf * 8, 128)), vm((nf * 8, 128)),
+            vm((nf * 8, 128)), vm((8, 128)),
             vm((2 * nf, 8, 128)), vm((nf, 8, 128)),
             vm((5, 8, 8, count)),
             vm((5, 8, 8, 8, count)), vm((9, 2, 8, 8, 128)),
-            dma((18,)), dma, dma,
+            dma((18,)), dma, dma, dma, dma,
             dma((2,)), dma((2,)), dma((2,)), dma((2,)), dma((2,)),
         ],
         compiler_params=pltpu.CompilerParams(

time: 50 us -> 49.3 us (0.986)
  Pallas kernels: 49.2 us -> 48.5 us
    pallas_call x1, Pallas kernels: 44.1 us -> 43.6 us  [root_call(): pl.pallas_call(functools.partial(root_kernel, (nf, ng, cx, cy, nz)), out_...]
where the time goes in v6:
time: 49.3 us; the launch traced here: 49.2 us
  Pallas kernels  48.5 us (98%)
  between operations  0.64 us (1%)
    pallas_call x1, Pallas kernels, root_call(): pl.pallas_call(functools.partial(root_kernel, (nf, ng, cx, cy, nz)), out_...  43.6 us
    pallas_call x1, Pallas kernels, root_call(): pl.pallas_call(patch_kernel, out_shape=(jax.ShapeDtypeStruct((8, 8, 8, co...  4.97 us

profile of v6, /device:TPU:1, one launch (start us, length us, event | category | flops | bytes accessed | tf_op | source)
XLA Modules:
  0.0 49.2 jit_solution(137140188885477895)
XLA Ops:
  0.6 43.6 %shard_map.184 = (f32[24,96,128]{2,1,0:T(8,128)}, f32[256,128]{1,0:T(8,128)}, f32[8,128]{1,0:T(8,128)}, f32[9,2,8,8,128]{4,3,2,1,0:T(8,128)}) custom-call(s32[2,64]{1,0:T(2,128)} %bitcast.1, f32[24,96,128]{2,1,0:T(8,128)} %rho.1, f32[5,12,12,12,32]{4,3,2,1,0:T(8,128)} %fluid_h.1, bf16[256,256]{1,0:T(8,128)(2,1)} %constant.28.clone.sz_h, ...), custom_call_target="tpu_custom_call" | custom-call | tf_op jit(solution)/shard_map/pallas_call | solution.py:891
  44.2 5.0 %shard_map.185 = (f32[8,8,8,32]{3,2,1,0:T(8,128)}, f32[5,8,8,8,32]{4,3,2,1,0:T(8,128)}, f32[24,96,128]{2,1,0:T(8,128)}) custom-call(f32[256,128]{1,0:T(8,128)} %get-tuple-element.10.blocks, f32[8,128]{1,0:T(8,128)} %get-tuple-element.11.most, f32[9,2,8,8,128]{4,3,2,1,0:T(8,128)} %get-tuple-element.12.packed_h, f32[24,96,128]{2,1,0:T(8,128)} %get-tuple-element.13.pot_in, ...), custom_call_target="tpu_custom_call" | custom-call | tf_op jit(solution)/shard_map/pallas_call | solution.py:925

commit v7 on v6

--- a/solution.py
+++ b/solution.py
@@ -793,6 +793,18 @@
 
     copy_in.wait()
     copy_out.start()
+    needs[1].wait()
+
+    def spill(target, r, y, value):
+        for i in range(groups):
+            target[2 * i + r, y] = value[:, count * i : count * (i + 1)]
+
+    copies = [pltpu.make_async_copy(fine, fine_h, sems.at[2])] + [
+        pltpu.make_async_copy(moved.at[v], moved_h.at[v], sems.at[3 + v]) for v in range(5)
+    ]
+    for r, y in keys:
+        spill(moved.at[0], r, y, packed[4, r, y])
+    copies[1].start()
 
     def beside(old, r, y):
         other = old[1 - r, y]
@@ -830,21 +842,10 @@
     out = lax.fori_loop(0, SWEEPS, sweep, tuple(states[k] for k in keys))
     states = dict(zip(keys, out))
 
-    def spill(target, r, y, value):
-        for i in range(groups):
-            target[2 * i + r, y] = value[:, count * i : count * (i + 1)]
-
-    copies = [pltpu.make_async_copy(fine, fine_h, sems.at[2])] + [
-        pltpu.make_async_copy(moved.at[v], moved_h.at[v], sems.at[3 + v]) for v in range(5)
-    ]
     for r, y in keys:
         spill(fine, r, y, states[r, y])
     copies[0].start()
 
-    needs[1].wait()
-    for r, y in keys:
-        spill(moved.at[0], r, y, packed[4, r, y])
-    copies[1].start()
     step = COURANT * FINE_STEP / most[pl.ds(0, 1), :]
     work = {}
     for n in range(3):

time: 49.3 us -> 49.5 us (level)
  no operation moved by 1% of the time
where the time goes in v7:
time: 49.5 us; the launch traced here: 49.3 us
  Pallas kernels  48.7 us (98%)
  between operations  0.64 us (1%)
    pallas_call x1, Pallas kernels, root_call(): pl.pallas_call(functools.partial(root_kernel, (nf, ng, cx, cy, nz)), out_...  43.6 us
    pallas_call x1, Pallas kernels, root_call(): pl.pallas_call(patch_kernel, out_shape=(jax.ShapeDtypeStruct((8, 8, 8, co...  5.11 us

profile of v7, /device:TPU:1, one launch (start us, length us, event | category | flops | bytes accessed | tf_op | source)
XLA Modules:
  0.0 49.3 jit_solution(8193198635838485915)
XLA Ops:
  0.6 43.6 %shard_map.184 = (f32[24,96,128]{2,1,0:T(8,128)}, f32[256,128]{1,0:T(8,128)}, f32[8,128]{1,0:T(8,128)}, f32[9,2,8,8,128]{4,3,2,1,0:T(8,128)}) custom-call(s32[2,64]{1,0:T(2,128)} %bitcast.1, f32[24,96,128]{2,1,0:T(8,128)} %rho.1, f32[5,12,12,12,32]{4,3,2,1,0:T(8,128)} %fluid_h.1, bf16[256,256]{1,0:T(8,128)(2,1)} %constant.28.clone.sz_h, ...), custom_call_target="tpu_custom_call" | custom-call | tf_op jit(solution)/shard_map/pallas_call | solution.py:892
  44.2 5.1 %shard_map.185 = (f32[8,8,8,32]{3,2,1,0:T(8,128)}, f32[5,8,8,8,32]{4,3,2,1,0:T(8,128)}, f32[24,96,128]{2,1,0:T(8,128)}) custom-call(f32[256,128]{1,0:T(8,128)} %get-tuple-element.10.blocks, f32[8,128]{1,0:T(8,128)} %get-tuple-element.11.most, f32[9,2,8,8,128]{4,3,2,1,0:T(8,128)} %get-tuple-element.12.packed_h, f32[24,96,128]{2,1,0:T(8,128)} %get-tuple-element.13.pot_in, ...), custom_call_target="tpu_custom_call" | custom-call | tf_op jit(solution)/shard_map/pallas_call | solution.py:926
